TPU v7x, 32 devices: a whole 2x2x4 slice. The times are simulated.
32 devices in a mesh: sector: 4 (over y, core), dom: 8 (over z, x).
Axes of the slice: x: 2, y: 2, z: 4, core: 2. Of those that a mesh axis runs over, the one named last changes fastest.
Arguments:
- amplitudes: float32 [64, 48], replicated, may hold values from -0.3 to 0.3
- mode_shapes: float32 [48, 3, 32768], P(None, None, ('sector', 'dom')), may hold values from -6 to 6
- shape_grads: float32 [8, 3, 32768], P(None, None, ('sector', 'dom')), may hold values from -2.4 to 2.4
- lame_params: float32 [2, 32768], P(None, ('sector', 'dom')), may hold values from 0.5 to 2
- connectivity: int32 [8, 32768], P(None, ('sector', 'dom')), may hold values from -1 to 1791, as said below
- dom_sends: int32 [2, 8192], P(None, ('sector', 'dom')), may hold values from -1 to 1023, as said below
- sector_sends: int32 [2, 4096], P(None, ('sector', 'dom')), may hold values from -1 to 1023, as said below
Outputs:
- nodal_force: float32 [64, 3, 32768], P(None, None, ('sector', 'dom'))
- modal_force: float32 [64, 48], replicated
Inputs may be any that keep to these rules, and one draw needn't show every extreme that they name: `connectivity`: in each device's block, the live elements come first and the padding element slots after them hold -1 in all 8 rows; a live slot names a slot of the device's extended table. Some device has all 1024 slots live. `dom_sends`: each device's row lists its own node numbers first, then -1; a row holds 128 to 256 live entries, and some row is full. `sector_sends`: each device's row lists its own node numbers first, then -1; a row holds 64 to 128 live entries, and some row is full.
All inputs are finite; a program needn't handle non-finite values.
Results may differ from a plain program's by a relative error of at most 0.0003.
Values sent between devices are 32-bit elements; how exact they have to be, the bound alone decides.
No kernel may reach another device: no remote copies, remote signals or barrier semaphores. Data moves between devices by JAX's collectives and lax.ppermute only.
A program may use at most 64 MiB of HBM per device.

v0:
```python
import math

import jax
import jax.numpy as jnp
from jax import lax
from jax.sharding import PartitionSpec as P


def padded(cells, sides, width, closed):
    for axis, dim in sides:
        count = lax.axis_size(axis)
        ends = count if closed else count - 1
        head = lax.slice_in_dim(cells, 0, width, axis=dim)
        tail = lax.slice_in_dim(cells, cells.shape[dim] - width, cells.shape[dim], axis=dim)
        cells = jnp.concatenate(
            [
                lax.ppermute(tail, axis, [(i, (i + 1) % count) for i in range(ends)]),
                cells,
                lax.ppermute(head, axis, [((i + 1) % count, i) for i in range(ends)]),
            ],
            axis=dim,
        )
    return cells


def take_slots(node_table, send_lists):
    slot_width = node_table.shape[1]
    slot_index = jnp.where(send_lists < 0, slot_width, send_lists).reshape(-1)
    return jnp.take(node_table, slot_index, axis=1, mode="fill", fill_value=0.0)


def add_slots(node_table, send_lists, add_values):
    slot_width = node_table.shape[1]
    slot_index = jnp.where(send_lists < 0, slot_width, send_lists).reshape(-1)
    return node_table.at[:, slot_index].add(add_values, mode="drop")


def element_forces(accum, extended, connect, gradients, lame):
    ext_width = extended.shape[1]
    combo_total = extended.shape[0] // 3
    elem_total = connect.shape[1]
    slot_index = jnp.where(connect < 0, ext_width, connect).reshape(-1)
    corners = jnp.take(extended, slot_index, axis=1, mode="fill", fill_value=0.0).reshape(
        combo_total, 3, 8, elem_total
    )
    gradient = jnp.zeros((combo_total, 3, 3, elem_total), extended.dtype)
    for corner in range(8):
        gradient = gradient + corners[:, :, None, corner, :] * gradients[corner][None, None, :, :]
    quadratic = jnp.sum(gradient[:, :, :, None, :] * gradient[:, :, None, :, :], axis=1)
    green_strain = 0.5 * (gradient + jnp.swapaxes(gradient, 1, 2) + quadratic)
    strain_trace = green_strain[:, 0, 0] + green_strain[:, 1, 1] + green_strain[:, 2, 2]
    identity = jnp.eye(3, dtype=extended.dtype)[None, :, :, None]
    stress = lame[0] * strain_trace[:, None, None, :] * identity + 2.0 * lame[1] * green_strain
    piola = stress + jnp.sum(gradient[:, :, :, None, :] * stress[:, None, :, :, :], axis=2)
    corner_forces = jnp.stack(
        [jnp.sum(piola * gradients[corner][None, None, :, :], axis=2) for corner in range(8)],
        axis=2,
    )
    return accum.at[:, slot_index].add(
        corner_forces.reshape(3 * combo_total, 8 * elem_total), mode="drop"
    )


def outer_ends(ext_rows, slot_width):
    return jnp.concatenate([ext_rows[:, :slot_width], ext_rows[:, 3 * slot_width :]], axis=1)


def local(amplitudes, mode_shapes, shape_grads, lame_params, connectivity, dom_sends, sector_sends):
    modes_total, _, node_total = mode_shapes.shape
    combo_total = amplitudes.shape[0]
    table_rows = 3 * combo_total
    dom_width = dom_sends.shape[1]
    sec_width = sector_sends.shape[1]
    flat_shapes = mode_shapes.reshape(modes_total, 3 * node_total)
    displaced = jnp.dot(
        amplitudes, flat_shapes, precision=lax.Precision.HIGHEST, preferred_element_type=jnp.float32
    ).reshape(table_rows, node_total)
    dom_ext = padded(take_slots(displaced, dom_sends), (("dom", 1),), dom_width, False)
    sec_ext = padded(take_slots(displaced, sector_sends), (("sector", 1),), sec_width, True)
    halo_moved = jnp.concatenate(
        [outer_ends(dom_ext, dom_width), outer_ends(sec_ext, sec_width)], axis=1
    )
    extended = jnp.concatenate([displaced, halo_moved], axis=1)
    ext_width = extended.shape[1]
    elem_total = connectivity.shape[1]
    block_size = math.gcd(elem_total, 256)
    turn_total = elem_total // block_size

    def one_block(turn_index, forces):
        first_col = turn_index * block_size
        connect_block = lax.dynamic_slice_in_dim(connectivity, first_col, block_size, 1)
        grads_block = lax.dynamic_slice_in_dim(shape_grads, first_col, block_size, 2)
        lame_block = lax.dynamic_slice_in_dim(lame_params, first_col, block_size, 1)
        return element_forces(forces, extended, connect_block, grads_block, lame_block)

    slot_forces = lax.fori_loop(
        0, turn_total, one_block, jnp.zeros((table_rows, ext_width), jnp.float32)
    )
    own_forces = slot_forces[:, :node_total]
    dom_back = slot_forces[:, node_total : node_total + 2 * dom_width]
    sec_back = slot_forces[:, node_total + 2 * dom_width :]
    dom_return = padded(dom_back, (("dom", 1),), dom_width, False)
    own_forces = add_slots(own_forces, dom_sends, outer_ends(dom_return, dom_width))
    sec_return = padded(sec_back, (("sector", 1),), sec_width, True)
    own_forces = add_slots(own_forces, sector_sends, outer_ends(sec_return, sec_width))
    partial_modal = lax.dot_general(
        own_forces.reshape(combo_total, 3 * node_total),
        flat_shapes,
        (((1,), (1,)), ((), ())),
        precision=lax.Precision.HIGHEST,
        preferred_element_type=jnp.float32,
    )
    modal_total = lax.psum(partial_modal, ("sector", "dom"))
    all_nodes = node_total * lax.axis_size("sector") * lax.axis_size("dom")
    return (
        own_forces.reshape(combo_total, 3, node_total),
        modal_total / math.sqrt(3.0 * all_nodes),
    )


def solution(mesh):
    placed = (
        P(),
        P(None, None, ("sector", "dom")),
        P(None, None, ("sector", "dom")),
        P(None, ("sector", "dom")),
        P(None, ("sector", "dom")),
        P(None, ("sector", "dom")),
        P(None, ("sector", "dom")),
    )
    return jax.shard_map(
        local,
        mesh=mesh,
        in_specs=placed,
        out_specs=(P(None, None, ("sector", "dom")), P()),
        check_vma=False,
    )
```

profile of v0, /device:TPU:0, one launch (start us, length us, event | category | flops | bytes accessed | tf_op | source)
XLA Modules:
  0.0 230.5 jit_solution(7521642724586355657)
XLA Ops:
  2.1 1.1 copy.105
  5.3 1.6 gather_fusion.1
  7.1 4.8 %collective-permute-start = (f32[192,256]{0,1:T(8,128)S(1)}, f32[192,256]{0,1:T(8,128)S(1)}, u32[]{:S(2)}, u32[]{:S(2)}) collective-permute-start(f32[192,256]{0,1:T(8,128)S(1)} %get-tuple-element.244), channel_id=1, source_target_pairs={{0,1},{1,2},{2,3},{3,4},{4,5},{5,6},{6,7},{8,9},{9,10},{10,11},{11... | collective-permute-start | bytes 589832 | tf_op jit(solution)/shard_map/ppermute | solution.py:17
  12.0 1.0 gather_fusion.2
  13.9 1.5 collective-permute-start.1
  15.4 2.1 collective-permute-done
  17.5 7.3 %collective-permute-done.1 = f32[192,256]{0,1:T(8,128)S(1)} collective-permute-done((f32[192,256]{0,1:T(8,128)S(1)}, f32[192,256]{0,1:T(8,128)S(1)}, u32[]{:S(2)}, u32[]{:S(2)}) %collective-permute-start.1) | collective-permute-done | bytes 196640 | tf_op jit(solution)/shard_map/ppermute | solution.py:19
  25.1 1.1 copy-done.1
  26.2 136.4 %while.15 = (s32[]{:T(128)}, f32[192,1792]{0,1:T(8,128)S(1)}, s32[8,1024]{1,0:T(8,128)S(1)}, f32[2,1024]{1,0:T(2,128)}, f32[192,1792]{0,1:T(8,128)}, /*index=5*/...) while((s32[]{:T(128)}, f32[192,1792]{0,1:T(8,128)S(1)}, ...), condition=%wide.region_12.13_spmd, body=%wide.region_0.12_spmd.sunk | while | flops 12415007 | bytes 49229240 | solution.py:96
  26.2 0.8 constant_dynamic-slice_fusion.12
  27.1 1.3 constant_dynamic-slice_fusion.11
  28.4 10.1 %gather_fusion = f32[2048,192]{1,0:T(8,128)} fusion(f32[192,1792]{0,1:T(8,128)} %get-tuple-element.414, s32[2048]{0:T(1024)S(1)} %broadcast_clamp_fusion.2), kind=kCustom, calls=%fused_computation.clone.1 | custom fusion | bytes 3153920 | tf_op jit(solution)/shard_map/while/body/eval_jaxpr/jit(_take)/gather | solution.py:43
  38.5 1.9 copy.147
  41.1 1.1 fusion.28
  44.2 0.9 copy.149
  45.7 1.8 copy.151
  47.6 12.6 %scatter_fusion = f32[192,1792]{0,1:T(8,128)S(1)} fusion(f32[192,1792]{0,1:T(8,128)S(1)} %get-tuple-element.394, s32[2048]{0:T(1024)S(1)} %bitcast.158, f32[2048,192]{1,0:T(8,128)} %copy.151), kind=kCustom, calls=%fused_computation.3.clone.1 | custom fusion | flops 393216 | bytes 4726784 | tf_op jit(solution)/shard_map/while/body/eval_jaxpr/scatter-add | solution.py:59
  60.3 0.8 constant_dynamic-slice_fusion.12
  61.2 1.4 constant_dynamic-slice_fusion.11
  62.6 10.1 %gather_fusion = f32[2048,192]{1,0:T(8,128)} fusion(f32[192,1792]{0,1:T(8,128)} %get-tuple-element.414, s32[2048]{0:T(1024)S(1)} %broadcast_clamp_fusion.2), kind=kCustom, calls=%fused_computation.clone.1 | custom fusion | bytes 3153920 | tf_op jit(solution)/shard_map/while/body/eval_jaxpr/jit(_take)/gather | solution.py:43
  72.6 1.9 copy.147
  75.2 1.1 fusion.28
  78.3 0.9 copy.149
  79.8 1.8 copy.151
  81.7 12.6 %scatter_fusion = f32[192,1792]{0,1:T(8,128)S(1)} fusion(f32[192,1792]{0,1:T(8,128)S(1)} %get-tuple-element.394, s32[2048]{0:T(1024)S(1)} %bitcast.158, f32[2048,192]{1,0:T(8,128)} %copy.151), kind=kCustom, calls=%fused_computation.3.clone.1 | custom fusion | flops 393216 | bytes 4726784 | tf_op jit(solution)/shard_map/while/body/eval_jaxpr/scatter-add | solution.py:59
  94.4 0.8 constant_dynamic-slice_fusion.12
  95.3 1.3 constant_dynamic-slice_fusion.11
  96.6 10.1 %gather_fusion = f32[2048,192]{1,0:T(8,128)} fusion(f32[192,1792]{0,1:T(8,128)} %get-tuple-element.414, s32[2048]{0:T(1024)S(1)} %broadcast_clamp_fusion.2), kind=kCustom, calls=%fused_computation.clone.1 | custom fusion | bytes 3153920 | tf_op jit(solution)/shard_map/while/body/eval_jaxpr/jit(_take)/gather | solution.py:43
  106.7 1.9 copy.147
  109.3 1.1 fusion.28
  112.4 0.9 copy.149
  113.9 1.8 copy.151
  115.8 12.6 %scatter_fusion = f32[192,1792]{0,1:T(8,128)S(1)} fusion(f32[192,1792]{0,1:T(8,128)S(1)} %get-tuple-element.394, s32[2048]{0:T(1024)S(1)} %bitcast.158, f32[2048,192]{1,0:T(8,128)} %copy.151), kind=kCustom, calls=%fused_computation.3.clone.1 | custom fusion | flops 393216 | bytes 4726784 | tf_op jit(solution)/shard_map/while/body/eval_jaxpr/scatter-add | solution.py:59
  129.4 1.4 constant_dynamic-slice_fusion.11
  130.8 10.1 %gather_fusion = f32[2048,192]{1,0:T(8,128)} fusion(f32[192,1792]{0,1:T(8,128)} %get-tuple-element.414, s32[2048]{0:T(1024)S(1)} %broadcast_clamp_fusion.2), kind=kCustom, calls=%fused_computation.clone.1 | custom fusion | bytes 3153920 | tf_op jit(solution)/shard_map/while/body/eval_jaxpr/jit(_take)/gather | solution.py:43
  140.8 1.9 copy.147
  143.4 1.1 fusion.28
  146.5 0.9 copy.149
  148.0 1.8 copy.151
  149.9 12.6 %scatter_fusion = f32[192,1792]{0,1:T(8,128)S(1)} fusion(f32[192,1792]{0,1:T(8,128)S(1)} %get-tuple-element.394, s32[2048]{0:T(1024)S(1)} %bitcast.158, f32[2048,192]{1,0:T(8,128)} %copy.151), kind=kCustom, calls=%fused_computation.3.clone.1 | custom fusion | flops 393216 | bytes 4726784 | tf_op jit(solution)/shard_map/while/body/eval_jaxpr/scatter-add | solution.py:59
  162.6 4.3 %collective-permute-start.4 = (f32[192,256]{0,1:T(8,128)S(1)}, f32[192,256]{0,1:T(8,128)S(1)}, u32[]{:S(2)}, u32[]{:S(2)}) collective-permute-start(f32[192,256]{0,1:T(8,128)S(1)} %get-tuple-element.241), channel_id=1, source_target_pairs={{0,1},{1,2},{2,3},{3,4},{4,5},{5,6},{6,7},{8,9},{9,10},{10,11},{11... | collective-permute-start | bytes 589832 | tf_op jit(solution)/shard_map/ppermute | solution.py:17
  166.9 1.3 collective-permute-start.5
  169.0 1.7 collective-permute-start.7
  170.8 7.6 %collective-permute-done.4 = f32[192,256]{0,1:T(8,128)S(1)} collective-permute-done((f32[192,256]{0,1:T(8,128)S(1)}, f32[192,256]{0,1:T(8,128)S(1)}, u32[]{:S(2)}, u32[]{:S(2)}) %collective-permute-start.4) | collective-permute-done | bytes 196640 | tf_op jit(solution)/shard_map/ppermute | solution.py:17
  178.4 3.8 %scatter_custom_fusion.1 = f32[192,1024]{0,1:T(8,128)S(1)} fusion(f32[192,1024]{0,1:T(8,128)S(1)} %slice.257, s32[512]{0:T(512)S(1)} %bitcast.167, f32[192,256]{0,1:T(8,128)S(1)} %collective-permute-done.5, f32[]{:T(128)} %constant.152, f32[192,256]{0,1:T(8,128)S(1)} %collective-permute-done.4), kind=kCustom, calls=%fused_computation.67 | custom fusion | flops 196608 | bytes 1310724 | tf_op jit(solution)/shard_map/scatter-add | solution.py:35
  182.2 3.0 %scatter_custom_fusion.2 = f32[192,1024]{0,1:T(8,128)S(1)} fusion(f32[192,1024]{0,1:T(8,128)S(1)} %scatter_custom_fusion.1, s32[256]{0:T(256)S(1)} %bitcast.170, f32[192,128]{0,1:T(8,128)} %collective-permute-done.7, f32[]{:T(128)} %constant.152, f32[192,128]{0,1:T(8,128)} %collective-permute-done.6), kind=kCustom, calls=%fused_computation.72 | custom fusion | flops 98304 | bytes 983044 | tf_op jit(solution)/shard_map/scatter-add | solution.py:35
  187.3 41.2 %psum.7 = f32[64,48]{0,1:T(8,128)S(1)} all-reduce(f32[64,48]{0,1:T(8,128)S(1)} %fusion.18), channel_id=1, replica_groups=mesh['sector'=4,'dom'=8] {'sector','dom'}, use_global_device_ids=true, to_apply=%region_15.16 | all-reduce | flops 3072 | bytes 24576 | tf_op jit(solution)/shard_map/psum | solution.py:113
  229.2 1.3 copy.92
  (178 shorter events, 22.3 us)
Async XLA Ops:
  0.6 3.4 %copy-start = (f32[64,48]{0,1:T(8,128)S(1)}, f32[64,48]{0,1:T(8,128)}, u32[]{:S(2)}) copy-start(f32[64,48]{0,1:T(8,128)} %param.9) | copy-start | bytes 36868
  3.2 0.8 copy-start.2
  6.9 5.1 %copy-start.5 = (s32[2,128]{1,0:T(2,128)S(1)}, s32[2,128]{1,0:T(2,128)}, u32[]{:S(2)}) copy-start(s32[2,128]{1,0:T(2,128)} %param.15) | copy-start | bytes 3076
  7.1 10.4 %collective-permute-start = (f32[192,256]{0,1:T(8,128)S(1)}, f32[192,256]{0,1:T(8,128)S(1)}, u32[]{:S(2)}, u32[]{:S(2)}) collective-permute-start(f32[192,256]{0,1:T(8,128)S(1)} %get-tuple-element.244), channel_id=1, source_target_pairs={{0,1},{1,2},{2,3},{3,4},{4,5},{5,6},{6,7},{8,9},{9,10},{10,11},{11... | collective-permute-start | bytes 589832 | tf_op jit(solution)/shard_map/ppermute | solution.py:17
  13.1 11.8 %collective-permute-start.3 = (f32[192,128]{0,1:T(8,128)S(1)}, f32[192,128]{0,1:T(8,128)S(1)}, u32[]{:S(2)}, u32[]{:S(2)}) collective-permute-start(f32[192,128]{0,1:T(8,128)S(1)} %get-tuple-element.245), channel_id=1, source_target_pairs={{8,0},{16,8},{24,16},{0,24},{9,1},{17,9},{25,17},{1,25},{10,2},{18... | collective-permute-start | bytes 294920 | tf_op jit(solution)/shard_map/ppermute | solution.py:19
  13.8 11.0 %collective-permute-start.2 = (f32[192,128]{0,1:T(8,128)S(1)}, f32[192,128]{0,1:T(8,128)S(1)}, u32[]{:S(2)}, u32[]{:S(2)}) collective-permute-start(f32[192,128]{0,1:T(8,128)S(1)} %get-tuple-element.246), channel_id=1, source_target_pairs={{0,8},{8,16},{16,24},{24,0},{1,9},{9,17},{17,25},{25,1},{2,10},{10... | collective-permute-start | bytes 294920 | tf_op jit(solution)/shard_map/ppermute | solution.py:17
  13.9 11.0 %collective-permute-start.1 = (f32[192,256]{0,1:T(8,128)S(1)}, f32[192,256]{0,1:T(8,128)S(1)}, u32[]{:S(2)}, u32[]{:S(2)}) collective-permute-start(f32[192,256]{0,1:T(8,128)S(1)} %get-tuple-element.243), channel_id=1, source_target_pairs={{1,0},{2,1},{3,2},{4,3},{5,4},{6,5},{7,6},{9,8},{10,9},{11,10},{12... | collective-permute-start | bytes 589832 | tf_op jit(solution)/shard_map/ppermute | solution.py:19
  15.4 10.8 %copy-start.4 = (s32[8,1024]{1,0:T(8,128)S(1)}, s32[8,1024]{1,0:T(8,128)}, u32[]{:S(2)}) copy-start(s32[8,1024]{1,0:T(8,128)} %param.13) | copy-start | bytes 98308
  24.9 1.2 copy-start.1
  162.6 15.8 %collective-permute-start.4 = (f32[192,256]{0,1:T(8,128)S(1)}, f32[192,256]{0,1:T(8,128)S(1)}, u32[]{:S(2)}, u32[]{:S(2)}) collective-permute-start(f32[192,256]{0,1:T(8,128)S(1)} %get-tuple-element.241), channel_id=1, source_target_pairs={{0,1},{1,2},{2,3},{3,4},{4,5},{5,6},{6,7},{8,9},{9,10},{10,11},{11... | collective-permute-start | bytes 589832 | tf_op jit(solution)/shard_map/ppermute | solution.py:17
  166.9 11.4 %collective-permute-start.5 = (f32[192,256]{0,1:T(8,128)S(1)}, f32[192,256]{0,1:T(8,128)S(1)}, u32[]{:S(2)}, u32[]{:S(2)}) collective-permute-start(f32[192,256]{0,1:T(8,128)S(1)} %get-tuple-element.242), channel_id=1, source_target_pairs={{1,0},{2,1},{3,2},{4,3},{5,4},{6,5},{7,6},{9,8},{10,9},{11,10},{12... | collective-permute-start | bytes 589832 | tf_op jit(solution)/shard_map/ppermute | solution.py:19
  169.0 13.2 %collective-permute-start.6 = (f32[192,128]{0,1:T(8,128)}, f32[192,128]{0,1:T(8,128)}, u32[]{:S(2)}, u32[]{:S(2)}) collective-permute-start(f32[192,128]{0,1:T(8,128)} %get-tuple-element.239), channel_id=1, source_target_pairs={{0,8},{8,16},{16,24},{24,0},{1,9},{9,17},{17,25},{25,1},{2,10},{10... | collective-permute-start | bytes 294920 | tf_op jit(solution)/shard_map/ppermute | solution.py:17
  169.0 13.2 %collective-permute-start.7 = (f32[192,128]{0,1:T(8,128)}, f32[192,128]{0,1:T(8,128)}, u32[]{:S(2)}, u32[]{:S(2)}) collective-permute-start(f32[192,128]{0,1:T(8,128)} %get-tuple-element.240), channel_id=1, source_target_pairs={{8,0},{16,8},{24,16},{0,24},{9,1},{17,9},{25,17},{1,25},{10,2},{18... | collective-permute-start | bytes 294920 | tf_op jit(solution)/shard_map/ppermute | solution.py:19
  185.5 1.1 copy-start.3
where the time goes:
time: 232 us; the launch traced here: 231 us
  local copies, waits for them, and re-layouts  87.5 us (38%)
  other arithmetic  66.7 us (29%)
  blocking collectives  41.2 us (18%)
  waiting for transfers between devices  17 us (7%)
  starting transfers between devices  14.4 us (6%)
    scatter-add x4, other arithmetic, element_forces(): accum.at[:, slot_index]  50.6 us
    gather x8, local copies, waits for them, and re-layouts, element_forces(): jnp.take(extended, slot_index, axis=1, mode='fill', fill_value=0.0)  47.8 us
    psum x1, blocking collectives, local(): modal_total = lax.psum(partial_modal, ('sector', 'dom'))  41.2 us
    ppermute x4, waiting for transfers between devices, padded(): lax.ppermute(tail, axis, [(i, (i + 1) % count) for i in range(ends)])  9.72 us
    ppermute x4, starting transfers between devices, padded(): lax.ppermute(tail, axis, [(i, (i + 1) % count) for i in range(ends)])  9.2 us
    reshape x4, local copies, waits for them, and re-layouts, element_forces(): corner_forces.reshape(3 * combo_total, 8 * elem_total)  7.39 us
    ppermute x4, waiting for transfers between devices, padded(): lax.ppermute(head, axis, [((i + 1) % count, i) for i in range(ends)])  7.33 us
    scatter-add x2, other arithmetic, add_slots(): return node_table.at[:, slot_index].add(add_values, mode='drop')  6.78 us
  transfers between devices with their start and end apart: 8, of which 3 were waited for; matrix products, arithmetic and copies ran while one was open for 2% of the time, Pallas kernels for 0%

commit v1 on v0

v1 whole, which is shorter than its diff:
```python
import functools
import math

import jax
import jax.numpy as jnp
from jax import lax
from jax.experimental import pallas as pl
from jax.experimental.pallas import tpu as pltpu
from jax.sharding import PartitionSpec as P

F32 = jnp.float32
BF16 = jnp.bfloat16
I16 = jnp.int16
MIB = 1 << 20
LANES = 256
NN = (((1,), (0,)), ((), ()))
NT = (((1,), (1,)), ((), ()))


def dot(a, b, dims):
    return lax.dot_general(a, b, dims, preferred_element_type=F32)


def split(x):
    hi = x.astype(BF16)
    return hi, (x - hi.astype(F32)).astype(BF16)


def partners(count, even_up):
    out = []
    for i in range(count):
        up = (i % 2 == 0) == even_up
        out.append((i, i + 1 if up else i - 1))
    return out


def swap(x, axis, even_up, closed):
    count = lax.axis_size(axis)
    pairs = [(i, j) for i, j in partners(count, even_up) if closed or 0 <= j < count]
    return lax.ppermute(x, axis, [(i, j % count) for i, j in pairs])


def send_rows(par_ref, dom_ref, sec_ref):
    dom_odd = par_ref[0] == 1
    sec_odd = par_ref[1] == 1
    d0, d1 = dom_ref[0:1, :], dom_ref[1:2, :]
    s0, s1 = sec_ref[0:1, :], sec_ref[1:2, :]
    return [
        jnp.where(dom_odd, d0, d1),
        jnp.where(dom_odd, d1, d0),
        jnp.where(sec_odd, s0, s1),
        jnp.where(sec_odd, s1, s0),
    ]


def one_hot(row, node_total):
    ids = lax.broadcasted_iota(jnp.int32, (node_total, row.shape[1]), 0)
    return jnp.where(ids == row, 1.0, 0.0).astype(BF16)


def packet_kernel(par_ref, shapes_ref, dom_ref, sec_ref, *out_refs):
    node_total = shapes_ref.shape[2]
    modes = shapes_ref.shape[1]
    hot = [one_hot(r, node_total) for r in send_rows(par_ref, dom_ref, sec_ref)]
    for i in range(3):
        hi, lo = split(shapes_ref[i])
        for h, o in zip(hot, out_refs):
            o[i * modes : (i + 1) * modes, :] = dot(hi, h, NN) + dot(lo, h, NN)


def build_kernel(par_ref, shapes_ref, conn_ref, grads_ref, wh_ref, wl_ref, own_ref,
                 conn_s, grad_s, cs, ghs, gls, ios, phi_h, phi_l, *, dom_width, sec_width):
    node_total = shapes_ref.shape[2]
    modes = shapes_ref.shape[1]
    chunks = wh_ref.shape[0]
    conn = conn_ref[...]
    corner = lax.broadcasted_iota(jnp.int32, conn.shape, 0)
    grads = [grads_ref[j] for j in range(3)]
    total = list(grads)
    drop = jnp.zeros(conn.shape, jnp.bool_)
    for s in range(1, 8):
        same = pltpu.roll(conn, 8 - s, 0) == conn
        drop = drop | (same & (corner >= 8 - s))
        total = [t + jnp.where(same, pltpu.roll(g, 8 - s, 0), 0.0) for t, g in zip(total, grads)]
    conn_s[...] = jnp.where(drop, -1, conn)
    for j in range(3):
        grad_s[j] = total[j]
    for i in range(3):
        hi, lo = split(shapes_ref[i])
        phi_h[i * modes : (i + 1) * modes, :] = hi
        phi_l[i * modes : (i + 1) * modes, :] = lo
    ios[...] = lax.broadcasted_iota(jnp.int32, (8, LANES), 0).astype(I16)
    dom_odd, sec_odd = par_ref[0], par_ref[1]
    first = node_total
    segments = [(0, node_total, 0)]
    for width, odd in ((dom_width, dom_odd), (sec_width, sec_odd)):
        segments.append((first, width, first + (1 - odd) * width))
        segments.append((first + width, width, first + odd * width))
        first += 2 * width
    unit = 4

    def chunk(t, carry):
        e0 = pl.multiple_of(t * LANES, LANES)
        for a in range(8):
            cs[a] = jnp.broadcast_to(conn_s[a : a + 1, pl.ds(e0, LANES)], (8, LANES)).astype(I16)
            for j in range(3):
                g = jnp.broadcast_to(grad_s[j, a : a + 1, pl.ds(e0, LANES)], (8, LANES))
                hi, lo = split(g)
                ghs[j * 8 + a] = hi
                gls[j * 8 + a] = lo

        for row0, rows, slot0 in segments:

            def block(s, carry, row0=row0, slot0=slot0):
                s0 = pl.multiple_of(s * (8 * unit), 8 * unit)
                for k in range(unit):
                    ids = ios[...] + (slot0 + s0 + 8 * k).astype(I16)
                    hi = [jnp.zeros((8, LANES), BF16)] * 3
                    lo = list(hi)
                    for a in range(8):
                        m = cs[a] == ids
                        for j in range(3):
                            hi[j] = jnp.where(m, ghs[j * 8 + a], hi[j])
                            lo[j] = jnp.where(m, gls[j * 8 + a], lo[j])
                    r = pl.ds(row0 + s0 + 8 * k, 8)
                    for j in range(3):
                        wh_ref[t, r, j * LANES : (j + 1) * LANES] = hi[j]
                        wl_ref[t, r, j * LANES : (j + 1) * LANES] = lo[j]
                return carry

            lax.fori_loop(0, rows // (8 * unit), block, 0)
        wh = wh_ref[t, 0:node_total, :]
        own_ref[t] = (
            dot(phi_h[...], wh, NN)
            + dot(phi_l[...], wh, NN)
            + dot(phi_h[...], wl_ref[t, 0:node_total, :], NN)
        )
        return carry

    lax.fori_loop(0, chunks, chunk, 0)


def element_kernel(amps_ref, lame_ref, own_ref, a_ref, b_ref, c_ref, d_ref, wh_ref, wl_ref,
                   ph_ref, pl_ref, modal_ref, hal_h, hal_l, disp):
    node_total = wh_ref.shape[1] - sum(r.shape[1] for r in (a_ref, b_ref, c_ref, d_ref))
    chunks = wh_ref.shape[0]
    modes, combos = amps_ref.shape
    col = 0
    for r in (a_ref, b_ref, c_ref, d_ref):
        hi, lo = split(r[...])
        hal_h[:, col : col + r.shape[1]] = hi
        hal_l[:, col : col + r.shape[1]] = lo
        col += r.shape[1]
    amp_h, amp_l = split(amps_ref[...].T)
    amp = jnp.concatenate([amp_h, amp_h, amp_l], axis=1)
    modal_ref[...] = jnp.zeros_like(modal_ref)

    def chunk(t, carry):
        e0 = pl.multiple_of(t * LANES, LANES)
        wh = wh_ref[t, node_total:, :]
        grad = (
            own_ref[t]
            + dot(hal_h[...], wh, NN)
            + dot(hal_l[...], wh, NN)
            + dot(hal_h[...], wl_ref[t, node_total:, :], NN)
        )
        gh, gl = split(grad)
        for i in range(3):
            r = slice(i * modes, (i + 1) * modes)
            disp[i] = dot(amp, jnp.concatenate([gh[r], gl[r], gh[r]], axis=0), NN)
        for half in range(LANES // 128):
            lam = jnp.broadcast_to(lame_ref[0:1, pl.ds(e0 + half * 128, 128)], (16, 128)) * 0.5
            mu = jnp.broadcast_to(lame_ref[1:2, pl.ds(e0 + half * 128, 128)], (16, 128))

            def rows(b, carry, half=half, lam=lam, mu=mu):
                r0 = pl.multiple_of(b * 16, 16)
                h = [
                    [disp[i, pl.ds(r0, 16), j * LANES + half * 128 : j * LANES + half * 128 + 128] for j in range(3)]
                    for i in range(3)
                ]
                s = {}
                for j in range(3):
                    for k in range(j, 3):
                        q = h[0][j] * h[0][k] + h[1][j] * h[1][k] + h[2][j] * h[2][k]
                        s[j, k] = (h[j][k] + h[k][j]) + q
                trace = lam * (s[0, 0] + s[1, 1] + s[2, 2])
                for j in range(3):
                    for k in range(j, 3):
                        v = mu * s[j, k]
                        v = v + trace if j == k else v
                        s[j, k] = s[k, j] = v
                for i in range(3):
                    for j in range(3):
                        p = s[i, j] + (h[i][0] * s[0, j] + h[i][1] * s[1, j] + h[i][2] * s[2, j])
                        hi, lo = split(p)
                        at = (t, pl.ds(i * combos + r0, 16), slice(j * LANES + half * 128, j * LANES + half * 128 + 128))
                        ph_ref[at] = hi
                        pl_ref[at] = lo
                return carry

            lax.fori_loop(0, combos // 16, rows, 0)
        acc = modal_ref[...]
        for i in range(3):
            r = slice(i * modes, (i + 1) * modes)
            c = slice(i * combos, (i + 1) * combos)
            both = dot(jnp.concatenate([gh[r], gl[r]], axis=0), ph_ref[t, c, :], NT)
            acc = acc + both[:modes] + both[modes:] + dot(gh[r], pl_ref[t, c, :], NT)
        modal_ref[...] = acc
        return carry

    lax.fori_loop(0, chunks, chunk, 0)


def force_rows(ph_ref, pl_ref, wh_ref, wl_ref, t, lo, hi):
    wh = wh_ref[t, lo:hi, :]
    return (
        dot(ph_ref[t], wh, NT) + dot(pl_ref[t], wh, NT) + dot(ph_ref[t], wl_ref[t, lo:hi, :], NT)
    )


def halo_kernel(ph_ref, pl_ref, wh_ref, wl_ref, *out_refs):
    chunks, slots, _ = wh_ref.shape
    first = slots - sum(o.shape[1] for o in out_refs)
    for o in out_refs:
        o[...] = jnp.zeros_like(o)

    def chunk(t, carry):
        part = force_rows(ph_ref, pl_ref, wh_ref, wl_ref, t, first, slots)
        col = 0
        for o in out_refs:
            o[...] += part[:, col : col + o.shape[1]]
            col += o.shape[1]
        return carry

    lax.fori_loop(0, chunks, chunk, 0)


def own_kernel(ph_ref, pl_ref, wh_ref, wl_ref, out_ref):
    node_total = out_ref.shape[1]
    out_ref[...] = jnp.zeros_like(out_ref)

    def chunk(t, carry):
        out_ref[...] += force_rows(ph_ref, pl_ref, wh_ref, wl_ref, t, 0, node_total)
        return carry

    lax.fori_loop(0, wh_ref.shape[0], chunk, 0)


def add_kernel(par_ref, own_ref, dom_ref, sec_ref, a_ref, b_ref, c_ref, d_ref, out_ref):
    node_total = own_ref.shape[1]
    combos = out_ref.shape[1]
    total = own_ref[...]
    for row, r in zip(send_rows(par_ref, dom_ref, sec_ref), (a_ref, b_ref, c_ref, d_ref)):
        hot = one_hot(row, node_total)
        hi, lo = split(r[...])
        total = total + dot(hi, hot, NT) + dot(lo, hot, NT)
    for i in range(3):
        out_ref[i] = total[i * combos : (i + 1) * combos]


def call(kernel, out_shape, args, scratch=(), vmem=24, smem=(), flops=0):
    vm = pl.BlockSpec(memory_space=pltpu.VMEM)
    sm = pl.BlockSpec(memory_space=pltpu.SMEM)
    many = isinstance(out_shape, (list, tuple))
    return pl.pallas_call(
        kernel,
        out_shape=out_shape,
        in_specs=[sm if i in smem else vm for i in range(len(args))],
        out_specs=[vm] * len(out_shape) if many else vm,
        scratch_shapes=list(scratch),
        compiler_params=pltpu.CompilerParams(vmem_limit_bytes=vmem * MIB),
        cost_estimate=pl.CostEstimate(flops=flops, bytes_accessed=1 << 20, transcendentals=0),
    )(*args)


def local(amplitudes, mode_shapes, shape_grads, lame_params, connectivity, dom_sends, sector_sends):
    modes, _, node_total = mode_shapes.shape
    combos = amplitudes.shape[0]
    elems = connectivity.shape[1]
    dom_width, sec_width = dom_sends.shape[1], sector_sends.shape[1]
    slots = node_total + 2 * (dom_width + sec_width)
    chunks = elems // LANES
    cols = 3 * LANES
    sds = jax.ShapeDtypeStruct
    widths = (dom_width, dom_width, sec_width, sec_width)
    parity = jnp.stack([lax.axis_index("dom") % 2, lax.axis_index("sector") % 2]).astype(jnp.int32)
    shapes = mode_shapes.transpose(1, 0, 2)
    grads = shape_grads.transpose(1, 0, 2)

    def exchange(a, b, c, d):
        return (
            swap(a, "dom", True, False),
            swap(b, "dom", False, False),
            swap(c, "sector", True, True),
            swap(d, "sector", False, True),
        )

    packets = call(
        packet_kernel,
        [sds((3 * modes, w), F32) for w in widths],
        (parity, shapes, dom_sends, sector_sends),
        smem=(0,),
    )
    halo = exchange(*packets)
    wh, wl, own_grad = call(
        functools.partial(build_kernel, dom_width=dom_width, sec_width=sec_width),
        [sds((chunks, slots, cols), BF16)] * 2 + [sds((chunks, 3 * modes, cols), F32)],
        (parity, shapes, connectivity, grads),
        scratch=[
            pltpu.VMEM((8, elems), jnp.int32),
            pltpu.VMEM((3, 8, elems), F32),
            pltpu.VMEM((8, 8, LANES), I16),
            pltpu.VMEM((24, 8, LANES), BF16),
            pltpu.VMEM((24, 8, LANES), BF16),
            pltpu.VMEM((8, LANES), I16),
            pltpu.VMEM((3 * modes, node_total), BF16),
            pltpu.VMEM((3 * modes, node_total), BF16),
        ],
        smem=(0,),
        flops=6 * 3 * modes * node_total * 3 * elems,
    )
    ph, pl_, modal = call(
        element_kernel,
        [sds((chunks, 3 * combos, cols), BF16)] * 2 + [sds((modes, combos), F32)],
        (amplitudes.T, lame_params, own_grad, *halo, wh, wl),
        scratch=[
            pltpu.VMEM((3 * modes, sum(widths)), BF16),
            pltpu.VMEM((3 * modes, sum(widths)), BF16),
            pltpu.VMEM((3, combos, cols), F32),
        ],
    )
    back = call(halo_kernel, [sds((3 * combos, w), F32) for w in widths], (ph, pl_, wh, wl))
    returned = exchange(*back)
    own = call(
        own_kernel,
        sds((3 * combos, node_total), F32),
        (ph, pl_, wh, wl),
        flops=6 * 3 * combos * node_total * 3 * elems,
    )
    forces = call(
        add_kernel,
        sds((3, combos, node_total), F32),
        (parity, own, dom_sends, sector_sends, *returned),
        smem=(0,),
    )
    for axis in ("sector", "dom"):
        count = lax.axis_size(axis)
        step = 1
        while step < count:
            modal = modal + lax.ppermute(modal, axis, [(i, i ^ step) for i in range(count)])
            step *= 2
    all_nodes = node_total * lax.axis_size("sector") * lax.axis_size("dom")
    return forces.transpose(1, 0, 2), modal.T / math.sqrt(3.0 * all_nodes)


def solution(mesh):
    placed = (
        P(),
        P(None, None, ("sector", "dom")),
        P(None, None, ("sector", "dom")),
        P(None, ("sector", "dom")),
        P(None, ("sector", "dom")),
        P(None, ("sector", "dom")),
        P(None, ("sector", "dom")),
    )
    return jax.shard_map(
        local,
        mesh=mesh,
        in_specs=placed,
        out_specs=(P(None, None, ("sector", "dom")), P()),
        check_vma=False,
    )
```

time: 232 us -> 77.8 us (0.34)
  local copies, waits for them, and re-layouts: 87.5 us -> 4.09 us
  other arithmetic: 66.7 us -> 0.71 us
  blocking collectives: 41.2 us -> 0 us
  Pallas kernels: 0 us -> 38.3 us
  starting transfers between devices: 14.4 us -> 17.6 us
    scatter-add x6 -> x0, other arithmetic: 57.4 us -> none  [the longest x4 50.6 us: element_forces(): accum.at[:, slot_index]]
    gather x10 -> x0, local copies, waits for them, and re-layouts: 50.3 us -> none  [the longest x8 47.8 us: element_forces(): jnp.take(extended, slot_index, axis=1, mode='fill', fill_value=0.0)]
    psum x1 -> x0, blocking collectives: 41.2 us -> none  [local(): modal_total = lax.psum(partial_modal, ('sector', 'dom'))]
    pallas_call x0 -> x6, Pallas kernels: none -> 38.3 us  [call(): pl.pallas_call(kernel, out_shape=out_shape, in_specs=[sm if i in smem els...]
    slice x17 -> x0, local copies, waits for them, and re-layouts: 13.7 us -> none  [the longest x4 5.3 us: element_forces(): gradients[corner][None, None, :, :]]
    reshape x9 -> x0, local copies, waits for them, and re-layouts: 9.63 us -> none  [the longest x4 7.39 us: element_forces(): corner_forces.reshape(3 * combo_total, 8 * elem_total)]
    while x40 -> x0, local copies, waits for them, and re-layouts: 5.35 us -> none
    another operation x8 -> x0, local copies, waits for them, and re-layouts: 3.72 us -> none  [element_forces(): jnp.stack([jnp.sum(piola * gradients[corner][None, None, :, :], axis=2) f...]
  transfers between devices with their start and end apart: 8 -> 13, of which waited for: 3 -> 6; matrix products, arithmetic and copies ran while one was open for 2% -> 1% of each run, Pallas kernels for 0% -> 32%
where the time goes in v1:
time: 77.8 us; the launch traced here: 77.5 us
  Pallas kernels  38.3 us (49%)
  starting transfers between devices  17.6 us (23%)
  waiting for transfers between devices  15.9 us (20%)
  local copies, waits for them, and re-layouts  4.09 us (5%)
  between operations  0.8 us (1%)
    pallas_call x6, Pallas kernels, call(): pl.pallas_call(kernel, out_shape=out_shape, in_specs=[sm if i in smem els...  38.3 us
    ppermute x5, starting transfers between devices, local(): lax.ppermute(modal, axis, [(i, i ^ step) for i in range(count)])  8.98 us
    ppermute x8, starting transfers between devices, swap(): return lax.ppermute(x, axis, [(i, j % count) for i, j in pairs])  8.67 us
    ppermute x5, waiting for transfers between devices, local(): lax.ppermute(modal, axis, [(i, i ^ step) for i in range(count)])  8.57 us
    ppermute x8, waiting for transfers between devices, swap(): return lax.ppermute(x, axis, [(i, j % count) for i, j in pairs])  7.32 us
    unnamed x18, local copies, waits for them, and re-layouts  4.09 us
  transfers between devices with their start and end apart: 13, of which 6 were waited for; matrix products, arithmetic and copies ran while one was open for 1% of the time, Pallas kernels for 32%

profile of v1, /device:TPU:0, one launch (start us, length us, event | category | flops | bytes accessed | tf_op | source)
XLA Modules:
  0.0 77.5 jit_solution(601230351963578592)
XLA Ops:
  0.6 0.1 pad_add_fusion.par_ref
  0.7 0.0 copy-start
  0.7 1.1 %copy-done = f32[48,3,1024]{2,0,1:T(8,128)S(1)} copy-done((f32[48,3,1024]{2,0,1:T(8,128)S(1)}, f32[48,3,1024]{2,0,1:T(8,128)}, u32[]{:S(2)}) %copy-start) | copy-done | bytes 589848
  1.8 0.0 copy-start.3
  1.8 0.7 copy-done.3
  2.5 0.7 copy-done.5
  3.1 2.3 %shard_map.87 = (f32[144,256]{1,0:T(8,128)S(1)}, f32[144,256]{1,0:T(8,128)S(1)}, f32[144,128]{1,0:T(8,128)S(1)}, f32[144,128]{1,0:T(8,128)S(1)}) custom-call(s32[2]{0:T(128)S(1)} %pad_add_fusion.par_ref, f32[3,48,1024]{2,1,0:T(8,128)S(1)} %bitcast.8, s32[2,256]{1,0:T(2,128)S(1)} %copy-done.3, s32[2,128]{1,0:T(2,128)S(1)} %copy-done.5), custom_call_target="tpu_custom_call" | custom-call | bytes 1048576 | tf_op jit(solution)/shard_map/pallas_call | solution.py:265
  5.4 0.5 collective-permute-start.2
  5.9 2.6 %collective-permute-start.3 = (f32[144,128]{1,0:T(8,128)S(1)}, f32[144,128]{1,0:T(8,128)S(1)}, u32[]{:S(2)}, u32[]{:S(2)}) collective-permute-start(f32[144,128]{1,0:T(8,128)S(1)} %get-tuple-element.20), channel_id=1, source_target_pairs={{0,24},{8,16},{16,8},{24,0},{1,25},{9,17},{17,9},{25,1},{2,26},{10... | collective-permute-start | bytes 221192 | tf_op jit(solution)/shard_map/ppermute | solution.py:40
  8.6 1.5 %collective-permute-start = (f32[144,256]{1,0:T(8,128)S(1)}, f32[144,256]{1,0:T(8,128)S(1)}, u32[]{:S(2)}, u32[]{:S(2)}) collective-permute-start(f32[144,256]{1,0:T(8,128)S(1)} %get-tuple-element.17), channel_id=1, source_target_pairs={{0,1},{1,0},{2,3},{3,2},{4,5},{5,4},{6,7},{7,6},{8,9},{9,8},{10,11... | collective-permute-start | bytes 442376 | tf_op jit(solution)/shard_map/ppermute | solution.py:40
  10.1 0.7 collective-permute-start.1
  10.7 0.0 copy-start.7
  10.7 0.9 %copy-done.7 = f32[8,3,1024]{2,0,1:T(8,128)S(1)} copy-done((f32[8,3,1024]{2,0,1:T(8,128)S(1)}, f32[8,3,1024]{2,0,1:T(8,128)}, u32[]{:S(2)}) %copy-start.7) | copy-done | bytes 98328
  11.6 0.8 copy-done.8
  12.4 13.0 %shard_map.86 = (bf16[4,1792,768]{2,1,0:T(8,128)(2,1)S(1)}, bf16[4,1792,768]{2,1,0:T(8,128)(2,1)S(1)}, f32[4,144,768]{2,1,0:T(8,128)S(1)}) custom-call(s32[2]{0:T(128)S(1)} %pad_add_fusion.par_ref, f32[3,48,1024]{2,1,0:T(8,128)S(1)} %bitcast.9, s32[8,1024]{1,0:T(8,128)S(1)} %copy-done.8, f32[3,8,1024]{2,1,0:T(8,128)S(1)} %bitcast.11), custom_call_target="tpu_custom_call" | custom-call | flops 2717908992 | bytes 1048576 | tf_op jit(solution)/shard_map/pallas_call | solution.py:265
  25.4 0.0 collective-permute-done.2.c_ref
  25.4 0.0 collective-permute-done.3.d_ref
  25.4 0.0 collective-permute-done.a_ref
  25.4 0.0 collective-permute-done.1.b_ref
  25.4 0.0 copy-done.1
  25.4 0.0 copy-done.2
  25.4 8.3 %shard_map.88 = (bf16[4,192,768]{2,1,0:T(8,128)(2,1)S(1)}, bf16[4,192,768]{2,1,0:T(8,128)(2,1)S(1)}, f32[48,64]{1,0:T(8,128)S(1)}) custom-call(f32[48,64]{1,0:T(8,128)S(1)} %bitcast.10, f32[2,1024]{1,0:T(2,128)S(1)} %copy-done.2, f32[4,144,768]{2,1,0:T(8,128)S(1)} %get-tuple-element.16.own_ref, f32[144,256]{1,0:T(8,128)S(1)} %collective-permute-done.a_ref, ...), custom_call_target="tpu_custom_call" | custom-call | bytes 1048576 | tf_op jit(solution)/shard_map/pallas_call | solution.py:265
  33.8 0.0 collective-permute-start.8
  33.8 1.2 %collective-permute-done.8 = f32[48,64]{1,0:T(8,128)S(1)} collective-permute-done((f32[48,64]{1,0:T(8,128)S(1)}, f32[48,64]{1,0:T(8,128)S(1)}, u32[]{:S(2)}, u32[]{:S(2)}) %collective-permute-start.8) | collective-permute-done | bytes 12320 | tf_op jit(solution)/shard_map/ppermute | solution.py:350
  35.0 0.5 collective-permute-start.9
  35.5 3.3 %collective-permute-done.9 = f32[48,64]{1,0:T(8,128)S(1)} collective-permute-done((f32[48,64]{1,0:T(8,128)S(1)}, f32[48,64]{1,0:T(8,128)S(1)}, u32[]{:S(2)}, u32[]{:S(2)}) %collective-permute-start.9) | collective-permute-done | bytes 12320 | tf_op jit(solution)/shard_map/ppermute | solution.py:350
  38.8 4.3 %collective-permute-start.10 = (f32[48,64]{1,0:T(8,128)S(1)}, f32[48,64]{1,0:T(8,128)S(1)}, u32[]{:S(2)}, u32[]{:S(2)}) collective-permute-start(f32[48,64]{1,0:T(8,128)S(1)} %add.25), channel_id=1, source_target_pairs={{0,1},{1,0},{2,3},{3,2},{4,5},{5,4},{6,7},{7,6},{8,9},{9,8},{10,11... | collective-permute-start | bytes 36872 | tf_op jit(solution)/shard_map/ppermute | solution.py:350
  43.1 1.8 %collective-permute-done.10 = f32[48,64]{1,0:T(8,128)S(1)} collective-permute-done((f32[48,64]{1,0:T(8,128)S(1)}, f32[48,64]{1,0:T(8,128)S(1)}, u32[]{:S(2)}, u32[]{:S(2)}) %collective-permute-start.10) | collective-permute-done | bytes 12320 | tf_op jit(solution)/shard_map/ppermute | solution.py:350
  44.9 1.6 %collective-permute-start.11 = (f32[48,64]{1,0:T(8,128)S(1)}, f32[48,64]{1,0:T(8,128)S(1)}, u32[]{:S(2)}, u32[]{:S(2)}) collective-permute-start(f32[48,64]{1,0:T(8,128)S(1)} %add.26), channel_id=1, source_target_pairs={{0,2},{1,3},{2,0},{3,1},{4,6},{5,7},{6,4},{7,5},{8,10},{9,11},{10,... | collective-permute-start | bytes 36872 | tf_op jit(solution)/shard_map/ppermute | solution.py:350
  46.5 2.3 %collective-permute-done.11 = f32[48,64]{1,0:T(8,128)S(1)} collective-permute-done((f32[48,64]{1,0:T(8,128)S(1)}, f32[48,64]{1,0:T(8,128)S(1)}, u32[]{:S(2)}, u32[]{:S(2)}) %collective-permute-start.11) | collective-permute-done | bytes 12320 | tf_op jit(solution)/shard_map/ppermute | solution.py:350
  48.8 2.6 %collective-permute-start.12 = (f32[48,64]{1,0:T(8,128)S(1)}, f32[48,64]{1,0:T(8,128)S(1)}, u32[]{:S(2)}, u32[]{:S(2)}) collective-permute-start(f32[48,64]{1,0:T(8,128)S(1)} %add.27), channel_id=1, source_target_pairs={{0,4},{1,5},{2,6},{3,7},{4,0},{5,1},{6,2},{7,3},{8,12},{9,13},{10,... | collective-permute-start | bytes 36872 | tf_op jit(solution)/shard_map/ppermute | solution.py:350
  51.4 6.8 %shard_map.89.own_ref = f32[192,1024]{1,0:T(8,128)S(1)} custom-call(bf16[4,192,768]{2,1,0:T(8,128)(2,1)S(1)} %get-tuple-element.23.ph_ref, bf16[4,192,768]{2,1,0:T(8,128)(2,1)S(1)} %get-tuple-element.24.pl_ref, bf16[4,1792,768]{2,1,0:T(8,128)(2,1)S(1)} %get-tuple-element.21.wh_ref, bf16[4,1792,768]{2,1,0:T(8,128)(2,1)S(1)} %get-tuple-element.22.wl_ref), custom_call_target="tpu_custom_call" | custom-call | flops 3623878656 | bytes 1048576 | tf_op jit(solution)/shard_map/pallas_call | solution.py:265
  58.1 0.0 copy-start.4
  58.1 0.0 copy-start.6
  58.1 5.3 %shard_map.90 = (f32[192,256]{1,0:T(8,128)S(1)}, f32[192,256]{1,0:T(8,128)S(1)}, f32[192,128]{1,0:T(8,128)S(1)}, f32[192,128]{1,0:T(8,128)S(1)}) custom-call(bf16[4,192,768]{2,1,0:T(8,128)(2,1)S(1)} %get-tuple-element.23.ph_ref, bf16[4,192,768]{2,1,0:T(8,128)(2,1)S(1)} %get-tuple-element.24.pl_ref, bf16[4,1792,768]{2,1,0:T(8,128)(2,1)S(1)} %get-tuple-element.21.wh_ref, ...), custom_call_target="tpu_custom_call" | custom-call | bytes 1048576 | tf_op jit(solution)/shard_map/pallas_call | solution.py:265
  63.4 0.1 collective-permute-start.6
  63.5 0.6 collective-permute-start.7
  64.1 2.0 %collective-permute-start.4 = (f32[192,256]{1,0:T(8,128)S(1)}, f32[192,256]{1,0:T(8,128)S(1)}, u32[]{:S(2)}, u32[]{:S(2)}) collective-permute-start(f32[192,256]{1,0:T(8,128)S(1)} %get-tuple-element.25), channel_id=1, source_target_pairs={{0,1},{1,0},{2,3},{3,2},{4,5},{5,4},{6,7},{7,6},{8,9},{9,8},{10,11... | collective-permute-start | bytes 589832 | tf_op jit(solution)/shard_map/ppermute | solution.py:40
  66.1 0.7 collective-permute-start.5
  66.8 0.0 collective-permute-done.12
  66.8 0.6 multiply_bitcast_fusion
  67.4 0.0 collective-permute-done.6.c_ref
  67.4 0.7 collective-permute-done.7.d_ref
  68.1 6.6 %collective-permute-done.4.a_ref = f32[192,256]{1,0:T(8,128)S(1)} collective-permute-done((f32[192,256]{1,0:T(8,128)S(1)}, f32[192,256]{1,0:T(8,128)S(1)}, u32[]{:S(2)}, u32[]{:S(2)}) %collective-permute-start.4) | collective-permute-done | bytes 196640 | tf_op jit(solution)/shard_map/ppermute | solution.py:40
  74.7 0.0 collective-permute-done.5.b_ref
  74.8 0.0 copy-done.4
  74.8 0.0 copy-done.6
  74.8 2.7 %shard_map.91 = f32[3,64,1024]{2,1,0:T(8,128)} custom-call(s32[2]{0:T(128)S(1)} %pad_add_fusion.par_ref, f32[192,1024]{1,0:T(8,128)S(1)} %shard_map.89.own_ref, s32[2,256]{1,0:T(2,128)S(1)} %copy-done.4, s32[2,128]{1,0:T(2,128)S(1)} %copy-done.6, f32[192,256]{1,0:T(8,128)S(1)} %collective-permute-done.4.a_ref, f32[192,256]{1,0:T(8,128)S(1)} %collective-permute-done.5.b_ref, ...), custom_call_target="tpu_custom_call" | custom-call | bytes 1048576 | tf_op jit(solution)/shard_map/pallas_call | solution.py:265
  (8 shorter events, 0.0 us)
Async XLA Ops:
  0.7 1.1 %copy-start = (f32[48,3,1024]{2,0,1:T(8,128)S(1)}, f32[48,3,1024]{2,0,1:T(8,128)}, u32[]{:S(2)}) copy-start(f32[48,3,1024]{2,0,1:T(8,128)} %param.8) | copy-start | bytes 1769476
  1.8 0.7 copy-start.3
  2.5 0.7 copy-start.5
  5.4 20.0 %collective-permute-start.2 = (f32[144,128]{1,0:T(8,128)S(1)}, f32[144,128]{1,0:T(8,128)S(1)}, u32[]{:S(2)}, u32[]{:S(2)}) collective-permute-start(f32[144,128]{1,0:T(8,128)S(1)} %get-tuple-element.19), channel_id=1, source_target_pairs={{0,8},{8,0},{16,24},{24,16},{1,9},{9,1},{17,25},{25,17},{2,10},{10... | collective-permute-start | bytes 221192 | tf_op jit(solution)/shard_map/ppermute | solution.py:40
  5.9 19.4 %collective-permute-start.3 = (f32[144,128]{1,0:T(8,128)S(1)}, f32[144,128]{1,0:T(8,128)S(1)}, u32[]{:S(2)}, u32[]{:S(2)}) collective-permute-start(f32[144,128]{1,0:T(8,128)S(1)} %get-tuple-element.20), channel_id=1, source_target_pairs={{0,24},{8,16},{16,8},{24,0},{1,25},{9,17},{17,9},{25,1},{2,26},{10... | collective-permute-start | bytes 221192 | tf_op jit(solution)/shard_map/ppermute | solution.py:40
  8.6 16.8 %collective-permute-start = (f32[144,256]{1,0:T(8,128)S(1)}, f32[144,256]{1,0:T(8,128)S(1)}, u32[]{:S(2)}, u32[]{:S(2)}) collective-permute-start(f32[144,256]{1,0:T(8,128)S(1)} %get-tuple-element.17), channel_id=1, source_target_pairs={{0,1},{1,0},{2,3},{3,2},{4,5},{5,4},{6,7},{7,6},{8,9},{9,8},{10,11... | collective-permute-start | bytes 442376 | tf_op jit(solution)/shard_map/ppermute | solution.py:40
  10.1 15.3 %collective-permute-start.1 = (f32[144,256]{1,0:T(8,128)S(1)}, f32[144,256]{1,0:T(8,128)S(1)}, u32[]{:S(2)}, u32[]{:S(2)}) collective-permute-start(f32[144,256]{1,0:T(8,128)S(1)} %get-tuple-element.18), channel_id=1, source_target_pairs={{1,2},{2,1},{3,4},{4,3},{5,6},{6,5},{9,10},{10,9},{11,12},{12,11},... | collective-permute-start | bytes 442376 | tf_op jit(solution)/shard_map/ppermute | solution.py:40
  10.7 0.9 %copy-start.7 = (f32[8,3,1024]{2,0,1:T(8,128)S(1)}, f32[8,3,1024]{2,0,1:T(8,128)}, u32[]{:S(2)}) copy-start(f32[8,3,1024]{2,0,1:T(8,128)} %param.9) | copy-start | bytes 294916
  11.6 0.8 copy-start.8
  12.4 13.0 %copy-start.1 = (f32[64,48]{0,1:T(8,128)S(1)}, f32[64,48]{0,1:T(8,128)}, u32[]{:S(2)}) copy-start(f32[64,48]{0,1:T(8,128)} %param.7) | copy-start | bytes 36868
  12.4 13.0 %copy-start.2 = (f32[2,1024]{1,0:T(2,128)S(1)}, f32[2,1024]{1,0:T(2,128)}, u32[]{:S(2)}) copy-start(f32[2,1024]{1,0:T(2,128)} %lame_ref.1) | copy-start | bytes 24580
  33.8 1.2 %collective-permute-start.8 = (f32[48,64]{1,0:T(8,128)S(1)}, f32[48,64]{1,0:T(8,128)S(1)}, u32[]{:S(2)}, u32[]{:S(2)}) collective-permute-start(f32[48,64]{1,0:T(8,128)S(1)} %get-tuple-element.29), channel_id=1, source_target_pairs={{0,8},{8,0},{16,24},{24,16},{1,9},{9,1},{17,25},{25,17},{2,10},{10... | collective-permute-start | bytes 36872 | tf_op jit(solution)/shard_map/ppermute | solution.py:350
  35.0 3.8 %collective-permute-start.9 = (f32[48,64]{1,0:T(8,128)S(1)}, f32[48,64]{1,0:T(8,128)S(1)}, u32[]{:S(2)}, u32[]{:S(2)}) collective-permute-start(f32[48,64]{1,0:T(8,128)S(1)} %add.24), channel_id=1, source_target_pairs={{0,16},{8,24},{16,0},{24,8},{1,17},{9,25},{17,1},{25,9},{2,18},{10... | collective-permute-start | bytes 36872 | tf_op jit(solution)/shard_map/ppermute | solution.py:350
  38.8 6.1 %collective-permute-start.10 = (f32[48,64]{1,0:T(8,128)S(1)}, f32[48,64]{1,0:T(8,128)S(1)}, u32[]{:S(2)}, u32[]{:S(2)}) collective-permute-start(f32[48,64]{1,0:T(8,128)S(1)} %add.25), channel_id=1, source_target_pairs={{0,1},{1,0},{2,3},{3,2},{4,5},{5,4},{6,7},{7,6},{8,9},{9,8},{10,11... | collective-permute-start | bytes 36872 | tf_op jit(solution)/shard_map/ppermute | solution.py:350
  44.9 3.8 %collective-permute-start.11 = (f32[48,64]{1,0:T(8,128)S(1)}, f32[48,64]{1,0:T(8,128)S(1)}, u32[]{:S(2)}, u32[]{:S(2)}) collective-permute-start(f32[48,64]{1,0:T(8,128)S(1)} %add.26), channel_id=1, source_target_pairs={{0,2},{1,3},{2,0},{3,1},{4,6},{5,7},{6,4},{7,5},{8,10},{9,11},{10,... | collective-permute-start | bytes 36872 | tf_op jit(solution)/shard_map/ppermute | solution.py:350
  48.8 18.0 %collective-permute-start.12 = (f32[48,64]{1,0:T(8,128)S(1)}, f32[48,64]{1,0:T(8,128)S(1)}, u32[]{:S(2)}, u32[]{:S(2)}) collective-permute-start(f32[48,64]{1,0:T(8,128)S(1)} %add.27), channel_id=1, source_target_pairs={{0,4},{1,5},{2,6},{3,7},{4,0},{5,1},{6,2},{7,3},{8,12},{9,13},{10,... | collective-permute-start | bytes 36872 | tf_op jit(solution)/shard_map/ppermute | solution.py:350
  58.1 16.6 %copy-start.4 = (s32[2,256]{1,0:T(2,128)S(1)}, s32[2,256]{1,0:T(2,128)}, u32[]{:S(2)}) copy-start(s32[2,256]{1,0:T(2,128)} %dom_ref.3) | copy-start | bytes 6148
  58.1 16.6 %copy-start.6 = (s32[2,128]{1,0:T(2,128)S(1)}, s32[2,128]{1,0:T(2,128)}, u32[]{:S(2)}) copy-start(s32[2,128]{1,0:T(2,128)} %sec_ref.3) | copy-start | bytes 3076
  63.4 4.0 %collective-permute-start.6 = (f32[192,128]{1,0:T(8,128)S(1)}, f32[192,128]{1,0:T(8,128)S(1)}, u32[]{:S(2)}, u32[]{:S(2)}) collective-permute-start(f32[192,128]{1,0:T(8,128)S(1)} %get-tuple-element.27), channel_id=1, source_target_pairs={{0,8},{8,0},{16,24},{24,16},{1,9},{9,1},{17,25},{25,17},{2,10},{10... | collective-permute-start | bytes 294920 | tf_op jit(solution)/shard_map/ppermute | solution.py:40
  63.5 4.6 %collective-permute-start.7 = (f32[192,128]{1,0:T(8,128)S(1)}, f32[192,128]{1,0:T(8,128)S(1)}, u32[]{:S(2)}, u32[]{:S(2)}) collective-permute-start(f32[192,128]{1,0:T(8,128)S(1)} %get-tuple-element.28), channel_id=1, source_target_pairs={{0,24},{8,16},{16,8},{24,0},{1,25},{9,17},{17,9},{25,1},{2,26},{10... | collective-permute-start | bytes 294920 | tf_op jit(solution)/shard_map/ppermute | solution.py:40
  64.1 10.6 %collective-permute-start.4 = (f32[192,256]{1,0:T(8,128)S(1)}, f32[192,256]{1,0:T(8,128)S(1)}, u32[]{:S(2)}, u32[]{:S(2)}) collective-permute-start(f32[192,256]{1,0:T(8,128)S(1)} %get-tuple-element.25), channel_id=1, source_target_pairs={{0,1},{1,0},{2,3},{3,2},{4,5},{5,4},{6,7},{7,6},{8,9},{9,8},{10,11... | collective-permute-start | bytes 589832 | tf_op jit(solution)/shard_map/ppermute | solution.py:40
  66.1 8.6 %collective-permute-start.5 = (f32[192,256]{1,0:T(8,128)S(1)}, f32[192,256]{1,0:T(8,128)S(1)}, u32[]{:S(2)}, u32[]{:S(2)}) collective-permute-start(f32[192,256]{1,0:T(8,128)S(1)} %get-tuple-element.26), channel_id=1, source_target_pairs={{1,2},{2,1},{3,4},{4,3},{5,6},{6,5},{9,10},{10,9},{11,12},{12,11},... | collective-permute-start | bytes 589832 | tf_op jit(solution)/shard_map/ppermute | solution.py:40

commit v2 on v1

v2 whole, which is shorter than its diff:
```python
import functools
import math

import jax
import jax.numpy as jnp
from jax import lax
from jax.experimental import pallas as pl
from jax.experimental.pallas import tpu as pltpu
from jax.sharding import PartitionSpec as P

F32 = jnp.float32
BF16 = jnp.bfloat16
I16 = jnp.int16
MIB = 1 << 20
LANES = 256
NN = (((1,), (0,)), ((), ()))
NT = (((1,), (1,)), ((), ()))


def dot(a, b, dims):
    return lax.dot_general(a, b, dims, preferred_element_type=F32)


def split(x):
    hi = x.astype(BF16)
    return hi, (x - hi.astype(F32)).astype(BF16)


def partners(count, even_up):
    out = []
    for i in range(count):
        up = (i % 2 == 0) == even_up
        out.append((i, i + 1 if up else i - 1))
    return out


def swap(x, axis, even_up, closed):
    count = lax.axis_size(axis)
    pairs = [(i, j) for i, j in partners(count, even_up) if closed or 0 <= j < count]
    return lax.ppermute(x, axis, [(i, j % count) for i, j in pairs])


def parity():
    return lax.axis_index("dom") % 2, lax.axis_index("sector") % 2


def send_rows(dom_ref, sec_ref):
    dom_odd, sec_odd = (p == 1 for p in parity())
    d0, d1 = dom_ref[0:1, :], dom_ref[1:2, :]
    s0, s1 = sec_ref[0:1, :], sec_ref[1:2, :]
    return [
        jnp.where(dom_odd, d0, d1),
        jnp.where(dom_odd, d1, d0),
        jnp.where(sec_odd, s0, s1),
        jnp.where(sec_odd, s1, s0),
    ]


def one_hot(row, node_total):
    ids = lax.broadcasted_iota(jnp.int32, (node_total, row.shape[1]), 0)
    return jnp.where(ids == row, 1.0, 0.0).astype(BF16)


def packet_kernel(shapes_hbm, grads_hbm, conn_hbm, lame_hbm, dom_hbm, sec_hbm,
                  a_ref, b_ref, c_ref, d_ref, hot_ref, phi_ref, grads_ref, conn_ref, lame_ref,
                  shapes_ref, dom_ref, sec_ref, sems):
    pairs = [
        (dom_hbm, dom_ref),
        (sec_hbm, sec_ref),
        (shapes_hbm, shapes_ref),
        (grads_hbm, grads_ref),
        (conn_hbm, conn_ref),
        (lame_hbm, lame_ref),
    ]
    copies = [pltpu.make_async_copy(src, dst, sems.at[k]) for k, (src, dst) in enumerate(pairs)]
    for c in copies:
        c.start()
    node_total = shapes_ref.shape[2]
    modes = shapes_ref.shape[1]
    copies[0].wait()
    copies[1].wait()
    col = 0
    for row in send_rows(dom_ref, sec_ref):
        width = row.shape[1]
        hot_ref[:, col : col + width] = one_hot(row, node_total)
        col += width
    copies[2].wait()
    for i in range(3):
        hi, lo = split(shapes_ref[i])
        phi_ref[i * modes : (i + 1) * modes, :] = hi
        phi_ref[(3 + i) * modes : (4 + i) * modes, :] = lo
    half = 3 * modes
    col = 0
    for o in (a_ref, b_ref, c_ref, d_ref):
        width = o.shape[1]
        part = dot(phi_ref[...], hot_ref[:, col : col + width], NN)
        o[...] = part[:half] + part[half:]
        col += width
    for c in copies[3:]:
        c.wait()


def build_kernel(phi_ref, conn_ref, grads_ref, wh_ref, wl_ref, vh_ref, vl_ref, own_ref,
                 conn_s, grad_s, cs, ghs, gls, ios, bases, *, dom_width, sec_width):
    node_total = phi_ref.shape[1]
    half = phi_ref.shape[0] // 2
    chunks = wh_ref.shape[0]
    conn = conn_ref[...]
    corner = lax.broadcasted_iota(jnp.int32, conn.shape, 0)
    grads = [grads_ref[j] for j in range(3)]
    total = list(grads)
    drop = jnp.zeros(conn.shape, jnp.bool_)
    for s in range(1, 8):
        same = pltpu.roll(conn, 8 - s, 0) == conn
        drop = drop | (same & (corner >= 8 - s))
        total = [t + jnp.where(same, pltpu.roll(g, 8 - s, 0), 0.0) for t, g in zip(total, grads)]
    conn_s[...] = jnp.where(drop, -1, conn)
    for j in range(3):
        grad_s[j] = total[j]
    ios[...] = lax.broadcasted_iota(jnp.int32, (8, LANES), 0).astype(I16)
    run = 0
    first = node_total
    for width, odd in zip((dom_width, sec_width), parity()):
        for start in (first + (1 - odd) * width, first + odd * width):
            for k in range(width // sec_width):
                bases[run] = start + k * sec_width
                run += 1
        first += 2 * width
    runs_each = run // 3

    def units(hi_ref, lo_ref, t, row0, slot0, count):
        for k in range(count):
            ids = ios[...] + (slot0 + 8 * k).astype(I16)
            hi = [jnp.zeros((8, LANES), BF16)] * 3
            lo = list(hi)
            for a in range(8):
                m = cs[a] == ids
                for j in range(3):
                    hi[j] = jnp.where(m, ghs[j * 8 + a], hi[j])
                    lo[j] = jnp.where(m, gls[j * 8 + a], lo[j])
            r = pl.ds(row0 + 8 * k, 8)
            for j in range(3):
                hi_ref[t, r, j * LANES : (j + 1) * LANES] = hi[j]
                lo_ref[t, r, j * LANES : (j + 1) * LANES] = lo[j]

    unit = 8

    def chunk(t, carry):
        e0 = pl.multiple_of(t * LANES, LANES)
        for a in range(8):
            cs[a] = jnp.broadcast_to(conn_s[a : a + 1, pl.ds(e0, LANES)], (8, LANES)).astype(I16)
            for j in range(3):
                g = jnp.broadcast_to(grad_s[j, a : a + 1, pl.ds(e0, LANES)], (8, LANES))
                hi, lo = split(g)
                ghs[j * 8 + a] = hi
                gls[j * 8 + a] = lo

        def own_rows(s, carry):
            s0 = pl.multiple_of(s * (8 * unit), 8 * unit)
            units(wh_ref, wl_ref, t, s0, s0, unit)
            return carry

        lax.fori_loop(0, node_total // (8 * unit), own_rows, 0)

        def halo_rows(j, carry):
            col = pl.ds(pl.multiple_of(j * LANES, LANES), LANES)
            part = dot(phi_ref[...], wh_ref[t, :, col], NN)
            own_ref[t, :, col] = part[:half] + part[half:] + dot(phi_ref[0:half], wl_ref[t, :, col], NN)
            for k in range(runs_each):
                run = j * runs_each + k
                row0 = pl.multiple_of(run * sec_width, sec_width)
                units(vh_ref, vl_ref, t, row0, bases[run], sec_width // 8)
            return carry

        lax.fori_loop(0, 3, halo_rows, 0)
        return carry

    lax.fori_loop(0, chunks, chunk, 0)


def element_kernel(amps_ref, lame_ref, own_ref, a_ref, b_ref, c_ref, d_ref, vh_ref, vl_ref,
                   pio_ref, modal_ref, hal, disp, grad_h, grad_l):
    chunks = vh_ref.shape[0]
    modes, combos = amps_ref.shape
    half = 3 * modes
    col = 0
    for r in (a_ref, b_ref, c_ref, d_ref):
        hi, lo = split(r[...])
        hal[0:half, col : col + r.shape[1]] = hi
        hal[half:, col : col + r.shape[1]] = lo
        col += r.shape[1]
    amp_h, amp_l = split(amps_ref[...].T)
    amp = jnp.concatenate([amp_h, amp_h, amp_l], axis=1)

    def gradient(t):
        part = dot(hal[...], vh_ref[t], NN)
        grad = own_ref[t] + part[:half] + part[half:] + dot(hal[0:half], vl_ref[t], NN)
        gh, gl = split(grad)
        grad_h[t] = gh
        grad_l[t] = gl
        for i in range(3):
            r = slice(i * modes, (i + 1) * modes)
            disp[t, i] = dot(amp, jnp.concatenate([gh[r], gl[r], gh[r]], axis=0), NN)

    def stress(t):
        for side in range(LANES // 128):
            e0 = t * LANES + side * 128
            lam = jnp.broadcast_to(lame_ref[0:1, e0 : e0 + 128], (16, 128)) * 0.5
            mu = jnp.broadcast_to(lame_ref[1:2, e0 : e0 + 128], (16, 128))
            at = [slice(j * LANES + side * 128, j * LANES + side * 128 + 128) for j in range(3)]
            for r0 in range(0, combos, 16):
                h = [[disp[t, i, r0 : r0 + 16, at[j]] for j in range(3)] for i in range(3)]
                s = {}
                for j in range(3):
                    for k in range(j, 3):
                        q = h[0][j] * h[0][k] + h[1][j] * h[1][k] + h[2][j] * h[2][k]
                        s[j, k] = (h[j][k] + h[k][j]) + q
                trace = lam * (s[0, 0] + s[1, 1] + s[2, 2])
                for j in range(3):
                    for k in range(j, 3):
                        v = mu * s[j, k]
                        v = v + trace if j == k else v
                        s[j, k] = s[k, j] = v
                for i in range(3):
                    for j in range(3):
                        p = s[i, j] + (h[i][0] * s[0, j] + h[i][1] * s[1, j] + h[i][2] * s[2, j])
                        hi, lo = split(p)
                        pio_ref[t, i * combos + r0 : i * combos + r0 + 16, at[j]] = hi
                        pio_ref[t, (3 + i) * combos + r0 : (3 + i) * combos + r0 + 16, at[j]] = lo

    def project(t, acc):
        for i in range(3):
            r = slice(i * modes, (i + 1) * modes)
            c = slice(i * combos, (i + 1) * combos)
            low = slice((3 + i) * combos, (4 + i) * combos)
            both = dot(jnp.concatenate([grad_h[t, r], grad_l[t, r]], axis=0), pio_ref[t, c, :], NT)
            acc = acc + both[:modes] + both[modes:] + dot(grad_h[t, r], pio_ref[t, low, :], NT)
        return acc

    acc = jnp.zeros((modes, combos), F32)
    gradient(0)
    for t in range(chunks):
        if t + 1 < chunks:
            gradient(t + 1)
        stress(t)
        acc = project(t, acc)
    modal_ref[...] = acc


def force_rows(pio_ref, wh_ref, wl_ref, t):
    half = pio_ref.shape[1] // 2
    part = dot(pio_ref[t], wh_ref[t], NT)
    return part[:half] + part[half:] + dot(pio_ref[t, 0:half, :], wl_ref[t], NT)


def halo_kernel(pio_ref, wh_ref, wl_ref, after_ref, *out_refs):
    del after_ref
    chunks = wh_ref.shape[0]
    for o in out_refs:
        o[...] = jnp.zeros_like(o)

    def chunk(t, carry):
        part = force_rows(pio_ref, wh_ref, wl_ref, t)
        col = 0
        for o in out_refs:
            o[...] += part[:, col : col + o.shape[1]]
            col += o.shape[1]
        return carry

    lax.fori_loop(0, chunks, chunk, 0)


def sum_kernel(a_ref, b_ref, after_ref, out_ref):
    del after_ref
    out_ref[...] = a_ref[...] + b_ref[...]


def own_kernel(pio_ref, wh_ref, wl_ref, after_ref, out_ref):
    del after_ref
    out_ref[...] = jnp.zeros_like(out_ref)

    def chunk(t, carry):
        out_ref[...] += force_rows(pio_ref, wh_ref, wl_ref, t)
        return carry

    lax.fori_loop(0, wh_ref.shape[0], chunk, 0)


def add_kernel(own_ref, hot_ref, a_ref, b_ref, c_ref, d_ref, out_hbm, back, out_s, sems):
    node_total = own_ref.shape[1]
    rows = own_ref.shape[0]
    combos = rows // 3
    col = 0
    for r in (a_ref, b_ref, c_ref, d_ref):
        hi, lo = split(r[...])
        back[0:rows, col : col + r.shape[1]] = hi
        back[rows:, col : col + r.shape[1]] = lo
        col += r.shape[1]
    copies = []
    for k in range(sems.shape[0]):
        width = node_total // sems.shape[0]
        at = slice(k * width, (k + 1) * width)
        part = dot(back[...], hot_ref[at, :], NT)
        for i in range(3):
            r = slice(i * combos, (i + 1) * combos)
            low = slice(rows + i * combos, rows + (i + 1) * combos)
            out_s[i, :, at] = own_ref[r, at] + part[r] + part[low]
        copies.append(pltpu.make_async_copy(out_s.at[:, :, at], out_hbm.at[:, :, at], sems.at[k]))
        copies[-1].start()
    for c in copies:
        c.wait()


def call(kernel, out_shape, args, scratch=(), vmem=24, hbm_in=(), any_in=(), any_out=False, flops=0):
    vm = pl.BlockSpec(memory_space=pltpu.VMEM)
    hbm = pl.BlockSpec(memory_space=pltpu.HBM)
    anywhere = pl.BlockSpec(memory_space=pl.ANY)
    many = isinstance(out_shape, (list, tuple))
    out = anywhere if any_out else vm
    args = [pltpu.with_memory_space_constraint(x, pltpu.HBM) if i in hbm_in else x for i, x in enumerate(args)]
    return pl.pallas_call(
        kernel,
        out_shape=out_shape,
        in_specs=[hbm if i in hbm_in else anywhere if i in any_in else vm for i in range(len(args))],
        out_specs=[out] * len(out_shape) if many else out,
        scratch_shapes=list(scratch),
        compiler_params=pltpu.CompilerParams(vmem_limit_bytes=vmem * MIB),
        cost_estimate=pl.CostEstimate(flops=flops, bytes_accessed=1 << 20, transcendentals=0),
    )(*args)


def local(amplitudes, mode_shapes, shape_grads, lame_params, connectivity, dom_sends, sector_sends):
    modes, _, node_total = mode_shapes.shape
    combos = amplitudes.shape[0]
    elems = connectivity.shape[1]
    dom_width, sec_width = dom_sends.shape[1], sector_sends.shape[1]
    chunks = elems // LANES
    cols = 3 * LANES
    sds = jax.ShapeDtypeStruct
    widths = (dom_width, dom_width, sec_width, sec_width)
    shapes = mode_shapes.transpose(1, 0, 2)
    grads = shape_grads.transpose(1, 0, 2)

    def exchange(a, b, c, d):
        return (
            swap(a, "dom", True, False),
            swap(b, "dom", False, False),
            swap(c, "sector", True, True),
            swap(d, "sector", False, True),
        )

    halo_width = sum(widths)
    *packets, hot, phi, grads_v, conn_v, lame_v = call(
        packet_kernel,
        [sds((3 * modes, w), F32) for w in widths]
        + [
            sds((node_total, halo_width), BF16),
            sds((6 * modes, node_total), BF16),
            sds(grads.shape, F32),
            sds(connectivity.shape, jnp.int32),
            sds(lame_params.shape, F32),
        ],
        (shapes, grads, connectivity, lame_params, dom_sends, sector_sends),
        scratch=[
            pltpu.VMEM(shapes.shape, F32),
            pltpu.VMEM(dom_sends.shape, jnp.int32),
            pltpu.VMEM(sector_sends.shape, jnp.int32),
            pltpu.SemaphoreType.DMA((6,)),
        ],
        hbm_in=range(6),
    )
    halo = exchange(*packets)
    wh, wl, vh, vl, own_grad = call(
        functools.partial(build_kernel, dom_width=dom_width, sec_width=sec_width),
        [sds((chunks, node_total, cols), BF16)] * 2
        + [sds((chunks, halo_width, cols), BF16)] * 2
        + [sds((chunks, 3 * modes, cols), F32)],
        (phi, conn_v, grads_v),
        scratch=[
            pltpu.VMEM((8, elems), jnp.int32),
            pltpu.VMEM((3, 8, elems), F32),
            pltpu.VMEM((8, 8, LANES), I16),
            pltpu.VMEM((24, 8, LANES), BF16),
            pltpu.VMEM((24, 8, LANES), BF16),
            pltpu.VMEM((8, LANES), I16),
            pltpu.SMEM((halo_width // sec_width,), jnp.int32),
        ],
        flops=6 * 3 * modes * node_total * 3 * elems,
    )
    pio, modal = call(
        element_kernel,
        [sds((chunks, 6 * combos, cols), BF16), sds((modes, combos), F32)],
        (amplitudes.T, lame_v, own_grad, *halo, vh, vl),
        scratch=[
            pltpu.VMEM((6 * modes, halo_width), BF16),
            pltpu.VMEM((chunks, 3, combos, cols), F32),
            pltpu.VMEM((chunks, 3 * modes, cols), BF16),
            pltpu.VMEM((chunks, 3 * modes, cols), BF16),
        ],
    )
    steps = []
    for axis in ("sector", "dom"):
        count = lax.axis_size(axis)
        step = 1
        while step < count:
            steps.append((axis, [(i, i ^ step) for i in range(count)]))
            step *= 2

    def other(x, k):
        return lax.ppermute(x, *steps[k])

    modal = modal + other(modal, 0)
    across = other(modal, 1)
    back = call(
        halo_kernel,
        [sds((3 * combos, w), F32) for w in widths],
        (pio, vh, vl, modal),
        any_in=(3,),
    )
    modal = call(sum_kernel, sds(modal.shape, F32), (modal, across, back[3]), any_in=(2,))
    modal = modal + other(modal, 2)
    returned = exchange(*back)
    own = call(
        own_kernel,
        sds((3 * combos, node_total), F32),
        (pio, wh, wl, modal),
        any_in=(3,),
        flops=6 * 3 * combos * node_total * 3 * elems,
    )
    forces = call(
        add_kernel,
        sds((3, combos, node_total), F32),
        (own, hot, *returned),
        scratch=[
            pltpu.VMEM((6 * combos, halo_width), BF16),
            pltpu.VMEM((3, combos, node_total), F32),
            pltpu.SemaphoreType.DMA((4,)),
        ],
        any_out=True,
    )
    for k in range(3, len(steps)):
        modal = modal + other(modal, k)
    all_nodes = node_total * lax.axis_size("sector") * lax.axis_size("dom")
    return forces.transpose(1, 0, 2), modal.T / math.sqrt(3.0 * all_nodes)


def solution(mesh):
    placed = (
        P(),
        P(None, None, ("sector", "dom")),
        P(None, None, ("sector", "dom")),
        P(None, ("sector", "dom")),
        P(None, ("sector", "dom")),
        P(None, ("sector", "dom")),
        P(None, ("sector", "dom")),
    )
    return jax.shard_map(
        local,
        mesh=mesh,
        in_specs=placed,
        out_specs=(P(None, None, ("sector", "dom")), P()),
        check_vma=False,
    )
```

time: 77.8 us -> 54 us (0.69)
  waiting for transfers between devices: 15.9 us -> 3.37 us
  Pallas kernels: 38.3 us -> 30.3 us
  local copies, waits for them, and re-layouts: 4.09 us -> 0.01 us
  starting transfers between devices: 17.6 us -> 18.7 us
    pallas_call x6 -> x7, Pallas kernels: 38.3 us -> 30.3 us  [call(): pl.pallas_call(kernel, out_shape=out_shape, in_specs=[hbm if i in hbm_in...]
    ppermute x8, waiting for transfers between devices: 7.32 us -> 0.02 us  [swap(): return lax.ppermute(x, axis, [(i, j % count) for i, j in pairs])]
    ppermute x5, waiting for transfers between devices: 8.57 us -> 3.35 us  [other(): return lax.ppermute(x, *steps[k])]
    unnamed x18 -> x2, local copies, waits for them, and re-layouts: 4.09 us -> 0.01 us
    ppermute x8, starting transfers between devices: 8.67 us -> 9.65 us  [swap(): return lax.ppermute(x, axis, [(i, j % count) for i, j in pairs])]
  transfers between devices with their start and end apart: 13 -> 13, of which waited for: 6 -> 3; matrix products, arithmetic and copies ran while one was open for 1% -> 1% of each run, Pallas kernels for 32% -> 40%
where the time goes in v2:
time: 54 us; the launch traced here: 53.9 us
  Pallas kernels  30.3 us (56%)
  starting transfers between devices  18.7 us (35%)
  waiting for transfers between devices  3.37 us (6%)
  between operations  0.8 us (1%)
  other arithmetic  0.63 us (1%)
    pallas_call x7, Pallas kernels, call(): pl.pallas_call(kernel, out_shape=out_shape, in_specs=[hbm if i in hbm_in...  30.3 us
    ppermute x8, starting transfers between devices, swap(): return lax.ppermute(x, axis, [(i, j % count) for i, j in pairs])  9.65 us
    ppermute x5, starting transfers between devices, other(): return lax.ppermute(x, *steps[k])  9.06 us
    ppermute x5, waiting for transfers between devices, other(): return lax.ppermute(x, *steps[k])  3.35 us
  transfers between devices with their start and end apart: 13, of which 3 were waited for; matrix products, arithmetic and copies ran while one was open for 1% of the time, Pallas kernels for 40%

profile of v2, /device:TPU:0, one launch (start us, length us, event | category | flops | bytes accessed | tf_op | source)
XLA Modules:
  0.0 53.9 jit_solution(5760349793174171839)
XLA Ops:
  0.6 2.0 %shard_map.86 = (f32[144,256]{1,0:T(8,128)S(1)}, f32[144,256]{1,0:T(8,128)S(1)}, f32[144,128]{1,0:T(8,128)S(1)}, f32[144,128]{1,0:T(8,128)S(1)}, bf16[1024,768]{...) custom-call(f32[3,48,1024]{2,1,0:T(8,128)} %bitcast.8, ...), custom_call_target="tpu_custom_call" | custom-call | bytes 1048576 | tf_op jit(solution)/shard_map/pallas_call | solution.py:321
  2.6 0.5 collective-permute-start.2
  3.1 2.6 %collective-permute-start.3 = (f32[144,128]{1,0:T(8,128)S(1)}, f32[144,128]{1,0:T(8,128)S(1)}, u32[]{:S(2)}, u32[]{:S(2)}) collective-permute-start(f32[144,128]{1,0:T(8,128)S(1)} %get-tuple-element.30), channel_id=1, source_target_pairs={{0,24},{8,16},{16,8},{24,0},{1,25},{9,17},{17,9},{25,1},{2,26},{10... | collective-permute-start | bytes 221192 | tf_op jit(solution)/shard_map/ppermute | solution.py:40
  5.8 1.5 %collective-permute-start = (f32[144,256]{1,0:T(8,128)S(1)}, f32[144,256]{1,0:T(8,128)S(1)}, u32[]{:S(2)}, u32[]{:S(2)}) collective-permute-start(f32[144,256]{1,0:T(8,128)S(1)} %get-tuple-element.27), channel_id=1, source_target_pairs={{0,1},{1,0},{2,3},{3,2},{4,5},{5,4},{6,7},{7,6},{8,9},{9,8},{10,11... | collective-permute-start | bytes 442376 | tf_op jit(solution)/shard_map/ppermute | solution.py:40
  7.2 0.7 %collective-permute-start.1 = (f32[144,256]{1,0:T(8,128)S(1)}, f32[144,256]{1,0:T(8,128)S(1)}, u32[]{:S(2)}, u32[]{:S(2)}) collective-permute-start(f32[144,256]{1,0:T(8,128)S(1)} %get-tuple-element.28), channel_id=1, source_target_pairs={{1,2},{2,1},{3,4},{4,3},{5,6},{6,5},{9,10},{10,9},{11,12},{12,11},... | collective-permute-start | bytes 442376 | tf_op jit(solution)/shard_map/ppermute | solution.py:40
  7.9 0.0 copy-start
  7.9 12.5 %shard_map.87 = (bf16[4,1024,768]{2,1,0:T(8,128)(2,1)S(1)}, bf16[4,1024,768]{2,1,0:T(8,128)(2,1)S(1)}, bf16[4,768,768]{2,1,0:T(8,128)(2,1)S(1)}, bf16[4,768,768]{2,1,0:T(8,128)(2,1)S(1)}, f32[4,144,768]{2,1,0:T(8,128)S(1)}) custom-call(bf16[288,1024]{1,0:T(8,128)(2,1)S(1)} %get-tuple-element.23.phi_ref, s32[8,1024]{1,0:T(8,128)S(1)} %get-tuple-element.24.conn_ref, ...), custom_call_target="tpu_custom_call" | custom-call | flops 2717908992 | bytes 1048576 | tf_op jit(solution)/shard_map/pallas_call | solution.py:321
  20.4 0.0 collective-permute-done.2.c_ref
  20.5 0.0 collective-permute-done.3.d_ref
  20.5 0.0 collective-permute-done.a_ref
  20.5 0.0 collective-permute-done.1.b_ref
  20.5 0.0 copy-done
  20.5 5.1 %shard_map.88 = (bf16[4,384,768]{2,1,0:T(8,128)(2,1)S(1)}, f32[48,64]{1,0:T(8,128)S(1)}) custom-call(f32[48,64]{1,0:T(8,128)S(1)} %bitcast.6, f32[2,1024]{1,0:T(2,128)S(1)} %get-tuple-element.22.lame_ref, f32[4,144,768]{2,1,0:T(8,128)S(1)} %get-tuple-element.26.own_ref, f32[144,256]{1,0:T(8,128)S(1)} %collective-permute-done.a_ref, ...), custom_call_target="tpu_custom_call" | custom-call | bytes 1048576 | tf_op jit(solution)/shard_map/pallas_call | solution.py:321
  25.6 0.0 collective-permute-start.4
  25.6 1.2 %collective-permute-done.4 = f32[48,64]{1,0:T(8,128)S(1)} collective-permute-done((f32[48,64]{1,0:T(8,128)S(1)}, f32[48,64]{1,0:T(8,128)S(1)}, u32[]{:S(2)}, u32[]{:S(2)}) %collective-permute-start.4) | collective-permute-done | bytes 12320 | tf_op jit(solution)/shard_map/ppermute | solution.py:410
  26.8 0.5 collective-permute-start.5
  27.3 4.0 %shard_map.89 = (f32[192,256]{1,0:T(8,128)S(1)}, f32[192,256]{1,0:T(8,128)S(1)}, f32[192,128]{1,0:T(8,128)S(1)}, f32[192,128]{1,0:T(8,128)S(1)}) custom-call(bf16[4,384,768]{2,1,0:T(8,128)(2,1)S(1)} %get-tuple-element.33.pio_ref, bf16[4,768,768]{2,1,0:T(8,128)(2,1)S(1)} %get-tuple-element.31.vh_ref.wh_ref, ...), custom_call_target="tpu_custom_call" | custom-call | bytes 1048576 | tf_op jit(solution)/shard_map/pallas_call | solution.py:321
  31.3 0.0 collective-permute-done.5.b_ref
  31.3 4.3 %collective-permute-start.6 = (f32[48,64]{1,0:T(8,128)S(1)}, f32[48,64]{1,0:T(8,128)S(1)}, u32[]{:S(2)}, u32[]{:S(2)}) collective-permute-start(f32[48,64]{1,0:T(8,128)S(1)} %shard_map.90), channel_id=1, source_target_pairs={{0,1},{1,0},{2,3},{3,2},{4,5},{5,4},{6,7},{7,6},{8,9},{9,8},{10,11... | collective-permute-start | bytes 36872 | tf_op jit(solution)/shard_map/ppermute | solution.py:410
  35.7 1.8 %collective-permute-done.6 = f32[48,64]{1,0:T(8,128)S(1)} collective-permute-done((f32[48,64]{1,0:T(8,128)S(1)}, f32[48,64]{1,0:T(8,128)S(1)}, u32[]{:S(2)}, u32[]{:S(2)}) %collective-permute-start.6) | collective-permute-done | bytes 12320 | tf_op jit(solution)/shard_map/ppermute | solution.py:410
  37.5 1.6 %collective-permute-start.11 = (f32[48,64]{1,0:T(8,128)S(1)}, f32[48,64]{1,0:T(8,128)S(1)}, u32[]{:S(2)}, u32[]{:S(2)}) collective-permute-start(f32[48,64]{1,0:T(8,128)S(1)} %add.13.after_ref), channel_id=1, source_target_pairs={{0,2},{1,3},{2,0},{3,1},{4,6},{5,7},{6,4},{7,5},{8,10},{9,11},{10,... | collective-permute-start | bytes 36872 | tf_op jit(solution)/shard_map/ppermute | solution.py:410
  39.1 0.0 collective-permute-start.10
  39.1 1.7 %collective-permute-start.9 = (f32[192,128]{1,0:T(8,128)S(1)}, f32[192,128]{1,0:T(8,128)S(1)}, u32[]{:S(2)}, u32[]{:S(2)}) collective-permute-start(f32[192,128]{1,0:T(8,128)S(1)} %get-tuple-element.41), channel_id=1, source_target_pairs={{0,8},{8,0},{16,24},{24,16},{1,9},{9,1},{17,25},{25,17},{2,10},{10... | collective-permute-start | bytes 294920 | tf_op jit(solution)/shard_map/ppermute | solution.py:40
  40.7 2.0 %collective-permute-start.7 = (f32[192,256]{1,0:T(8,128)S(1)}, f32[192,256]{1,0:T(8,128)S(1)}, u32[]{:S(2)}, u32[]{:S(2)}) collective-permute-start(f32[192,256]{1,0:T(8,128)S(1)} %get-tuple-element.39), channel_id=1, source_target_pairs={{0,1},{1,0},{2,3},{3,2},{4,5},{5,4},{6,7},{7,6},{8,9},{9,8},{10,11... | collective-permute-start | bytes 589832 | tf_op jit(solution)/shard_map/ppermute | solution.py:40
  42.7 0.7 %collective-permute-start.8 = (f32[192,256]{1,0:T(8,128)S(1)}, f32[192,256]{1,0:T(8,128)S(1)}, u32[]{:S(2)}, u32[]{:S(2)}) collective-permute-start(f32[192,256]{1,0:T(8,128)S(1)} %get-tuple-element.40), channel_id=1, source_target_pairs={{1,2},{2,1},{3,4},{4,3},{5,6},{6,5},{9,10},{10,9},{11,12},{12,11},... | collective-permute-start | bytes 589832 | tf_op jit(solution)/shard_map/ppermute | solution.py:40
  43.4 0.0 collective-permute-done.11
  43.4 2.7 %collective-permute-start.12 = (f32[48,64]{1,0:T(8,128)S(1)}, f32[48,64]{1,0:T(8,128)S(1)}, u32[]{:S(2)}, u32[]{:S(2)}) collective-permute-start(f32[48,64]{1,0:T(8,128)S(1)} %add.14), channel_id=1, source_target_pairs={{0,4},{1,5},{2,6},{3,7},{4,0},{5,1},{6,2},{7,3},{8,12},{9,13},{10,... | collective-permute-start | bytes 36872 | tf_op jit(solution)/shard_map/ppermute | solution.py:410
  46.1 5.2 %shard_map.91.own_ref = f32[192,1024]{1,0:T(8,128)S(1)} custom-call(bf16[4,384,768]{2,1,0:T(8,128)(2,1)S(1)} %get-tuple-element.33.pio_ref, bf16[4,1024,768]{2,1,0:T(8,128)(2,1)S(1)} %get-tuple-element.34.wh_ref, bf16[4,1024,768]{2,1,0:T(8,128)(2,1)S(1)} %get-tuple-element.35.wl_ref, f32[48,64]{1,0:T(8,128)S(1)} %add.13.after_ref), custom_call_target="tpu_custom_call" | custom-call | flops 3623878656 | bytes 1048576 | tf_op jit(solution)/shard_map/pallas_call | solution.py:321
  51.3 0.3 collective-permute-done.12
  51.6 0.6 %multiply_bitcast_fusion = f32[64,48]{0,1:T(8,128)} fusion(f32[48,64]{1,0:T(8,128)S(1)} %add.14, f32[48,64]{1,0:T(8,128)S(1)} %collective-permute-done.12), kind=kLoop, calls=%fused_computation | loop fusion | flops 6144 | bytes 36864 | tf_op jit(solution)/shard_map/div | solution.py:444
  52.2 0.0 collective-permute-done.9.c_ref
  52.2 0.0 collective-permute-done.10.d_ref
  52.2 0.0 collective-permute-done.7.a_ref
  52.2 0.0 collective-permute-done.8.b_ref
  52.2 1.6 %shard_map.92 = f32[3,64,1024]{2,1,0:T(8,128)} custom-call(f32[192,1024]{1,0:T(8,128)S(1)} %shard_map.91.own_ref, bf16[1024,768]{1,0:T(8,128)(2,1)S(1)} %get-tuple-element.38.hot_ref, f32[192,256]{1,0:T(8,128)S(1)} %collective-permute-done.7.a_ref, f32[192,256]{1,0:T(8,128)S(1)} %collective-permute-done.8.b_ref, ...), custom_call_target="tpu_custom_call" | custom-call | bytes 1048576 | tf_op jit(solution)/shard_map/pallas_call | solution.py:321
  (4 shorter events, 0.0 us)
Async XLA Ops:
  2.6 17.9 %collective-permute-start.2 = (f32[144,128]{1,0:T(8,128)S(1)}, f32[144,128]{1,0:T(8,128)S(1)}, u32[]{:S(2)}, u32[]{:S(2)}) collective-permute-start(f32[144,128]{1,0:T(8,128)S(1)} %get-tuple-element.29), channel_id=1, source_target_pairs={{0,8},{8,0},{16,24},{24,16},{1,9},{9,1},{17,25},{25,17},{2,10},{10... | collective-permute-start | bytes 221192 | tf_op jit(solution)/shard_map/ppermute | solution.py:40
  3.1 17.3 %collective-permute-start.3 = (f32[144,128]{1,0:T(8,128)S(1)}, f32[144,128]{1,0:T(8,128)S(1)}, u32[]{:S(2)}, u32[]{:S(2)}) collective-permute-start(f32[144,128]{1,0:T(8,128)S(1)} %get-tuple-element.30), channel_id=1, source_target_pairs={{0,24},{8,16},{16,8},{24,0},{1,25},{9,17},{17,9},{25,1},{2,26},{10... | collective-permute-start | bytes 221192 | tf_op jit(solution)/shard_map/ppermute | solution.py:40
  5.8 14.7 %collective-permute-start = (f32[144,256]{1,0:T(8,128)S(1)}, f32[144,256]{1,0:T(8,128)S(1)}, u32[]{:S(2)}, u32[]{:S(2)}) collective-permute-start(f32[144,256]{1,0:T(8,128)S(1)} %get-tuple-element.27), channel_id=1, source_target_pairs={{0,1},{1,0},{2,3},{3,2},{4,5},{5,4},{6,7},{7,6},{8,9},{9,8},{10,11... | collective-permute-start | bytes 442376 | tf_op jit(solution)/shard_map/ppermute | solution.py:40
  7.2 13.2 %collective-permute-start.1 = (f32[144,256]{1,0:T(8,128)S(1)}, f32[144,256]{1,0:T(8,128)S(1)}, u32[]{:S(2)}, u32[]{:S(2)}) collective-permute-start(f32[144,256]{1,0:T(8,128)S(1)} %get-tuple-element.28), channel_id=1, source_target_pairs={{1,2},{2,1},{3,4},{4,3},{5,6},{6,5},{9,10},{10,9},{11,12},{12,11},... | collective-permute-start | bytes 442376 | tf_op jit(solution)/shard_map/ppermute | solution.py:40
  7.9 12.6 %copy-start = (f32[64,48]{0,1:T(8,128)S(1)}, f32[64,48]{0,1:T(8,128)}, u32[]{:S(2)}) copy-start(f32[64,48]{0,1:T(8,128)} %param.7) | copy-start | bytes 36868
  25.6 1.2 %collective-permute-start.4 = (f32[48,64]{1,0:T(8,128)S(1)}, f32[48,64]{1,0:T(8,128)S(1)}, u32[]{:S(2)}, u32[]{:S(2)}) collective-permute-start(f32[48,64]{1,0:T(8,128)S(1)} %get-tuple-element.36), channel_id=1, source_target_pairs={{0,8},{8,0},{16,24},{24,16},{1,9},{9,1},{17,25},{25,17},{2,10},{10... | collective-permute-start | bytes 36872 | tf_op jit(solution)/shard_map/ppermute | solution.py:410
  26.8 4.5 %collective-permute-start.5 = (f32[48,64]{1,0:T(8,128)S(1)}, f32[48,64]{1,0:T(8,128)S(1)}, u32[]{:S(2)}, u32[]{:S(2)}) collective-permute-start(f32[48,64]{1,0:T(8,128)S(1)} %add.12.after_ref.a_ref), channel_id=1, source_target_pairs={{0,16},{8,24},{16,0},{24,8},{1,17},{9,25},{17,1},{25,9},{2,18},{10... | collective-permute-start | bytes 36872 | tf_op jit(solution)/shard_map/ppermute | solution.py:410
  31.3 6.2 %collective-permute-start.6 = (f32[48,64]{1,0:T(8,128)S(1)}, f32[48,64]{1,0:T(8,128)S(1)}, u32[]{:S(2)}, u32[]{:S(2)}) collective-permute-start(f32[48,64]{1,0:T(8,128)S(1)} %shard_map.90), channel_id=1, source_target_pairs={{0,1},{1,0},{2,3},{3,2},{4,5},{5,4},{6,7},{7,6},{8,9},{9,8},{10,11... | collective-permute-start | bytes 36872 | tf_op jit(solution)/shard_map/ppermute | solution.py:410
  37.5 5.9 %collective-permute-start.11 = (f32[48,64]{1,0:T(8,128)S(1)}, f32[48,64]{1,0:T(8,128)S(1)}, u32[]{:S(2)}, u32[]{:S(2)}) collective-permute-start(f32[48,64]{1,0:T(8,128)S(1)} %add.13.after_ref), channel_id=1, source_target_pairs={{0,2},{1,3},{2,0},{3,1},{4,6},{5,7},{6,4},{7,5},{8,10},{9,11},{10,... | collective-permute-start | bytes 36872 | tf_op jit(solution)/shard_map/ppermute | solution.py:410
  39.1 13.2 %collective-permute-start.10 = (f32[192,128]{1,0:T(8,128)S(1)}, f32[192,128]{1,0:T(8,128)S(1)}, u32[]{:S(2)}, u32[]{:S(2)}) collective-permute-start(f32[192,128]{1,0:T(8,128)S(1)} %get-tuple-element.37.after_ref), channel_id=1, source_target_pairs={{0,24},{8,16},{16,8},{24,0},{1,25},{9,17},{17,9},{25,1},{2,26},{10... | collective-permute-start | bytes 294920 | tf_op jit(solution)/shard_map/ppermute | solution.py:40
  39.1 13.1 %collective-permute-start.9 = (f32[192,128]{1,0:T(8,128)S(1)}, f32[192,128]{1,0:T(8,128)S(1)}, u32[]{:S(2)}, u32[]{:S(2)}) collective-permute-start(f32[192,128]{1,0:T(8,128)S(1)} %get-tuple-element.41), channel_id=1, source_target_pairs={{0,8},{8,0},{16,24},{24,16},{1,9},{9,1},{17,25},{25,17},{2,10},{10... | collective-permute-start | bytes 294920 | tf_op jit(solution)/shard_map/ppermute | solution.py:40
  40.7 11.5 %collective-permute-start.7 = (f32[192,256]{1,0:T(8,128)S(1)}, f32[192,256]{1,0:T(8,128)S(1)}, u32[]{:S(2)}, u32[]{:S(2)}) collective-permute-start(f32[192,256]{1,0:T(8,128)S(1)} %get-tuple-element.39), channel_id=1, source_target_pairs={{0,1},{1,0},{2,3},{3,2},{4,5},{5,4},{6,7},{7,6},{8,9},{9,8},{10,11... | collective-permute-start | bytes 589832 | tf_op jit(solution)/shard_map/ppermute | solution.py:40
  42.7 9.5 %collective-permute-start.8 = (f32[192,256]{1,0:T(8,128)S(1)}, f32[192,256]{1,0:T(8,128)S(1)}, u32[]{:S(2)}, u32[]{:S(2)}) collective-permute-start(f32[192,256]{1,0:T(8,128)S(1)} %get-tuple-element.40), channel_id=1, source_target_pairs={{1,2},{2,1},{3,4},{4,3},{5,6},{6,5},{9,10},{10,9},{11,12},{12,11},... | collective-permute-start | bytes 589832 | tf_op jit(solution)/shard_map/ppermute | solution.py:40
  43.4 8.2 %collective-permute-start.12 = (f32[48,64]{1,0:T(8,128)S(1)}, f32[48,64]{1,0:T(8,128)S(1)}, u32[]{:S(2)}, u32[]{:S(2)}) collective-permute-start(f32[48,64]{1,0:T(8,128)S(1)} %add.14), channel_id=1, source_target_pairs={{0,4},{1,5},{2,6},{3,7},{4,0},{5,1},{6,2},{7,3},{8,12},{9,13},{10,... | collective-permute-start | bytes 36872 | tf_op jit(solution)/shard_map/ppermute | solution.py:410

commit v3 on v2

--- a/solution.py
+++ b/solution.py
@@ -100,11 +100,16 @@
         c.wait()
 
 
-def build_kernel(phi_ref, conn_ref, grads_ref, wh_ref, wl_ref, vh_ref, vl_ref, own_ref,
-                 conn_s, grad_s, cs, ghs, gls, ios, bases, *, dom_width, sec_width):
+def hold_kernel(x_ref, after_ref, out_ref):
+    del x_ref, after_ref, out_ref
+
+
+def build_kernel(phi_ref, conn_ref, grads_ref, *refs, dom_width, sec_width, chunks):
+    wh, wl, vh, vl = (refs[k * chunks : (k + 1) * chunks] for k in range(4))
+    own_ref, conn_s, grad_s, cs, ghs, gls, ios, phi_s, bases = refs[4 * chunks :]
+    phi_s[...] = phi_ref[...]
     node_total = phi_ref.shape[1]
     half = phi_ref.shape[0] // 2
-    chunks = wh_ref.shape[0]
     conn = conn_ref[...]
     corner = lax.broadcasted_iota(jnp.int32, conn.shape, 0)
     grads = [grads_ref[j] for j in range(3)]
@@ -118,69 +123,74 @@
     for j in range(3):
         grad_s[j] = total[j]
     ios[...] = lax.broadcasted_iota(jnp.int32, (8, LANES), 0).astype(I16)
+    stretch = sec_width // 2
     run = 0
     first = node_total
     for width, odd in zip((dom_width, sec_width), parity()):
         for start in (first + (1 - odd) * width, first + odd * width):
-            for k in range(width // sec_width):
-                bases[run] = start + k * sec_width
+            for k in range(width // stretch):
+                bases[run] = start + k * stretch
                 run += 1
         first += 2 * width
-    runs_each = run // 3
-
-    def units(hi_ref, lo_ref, t, row0, slot0, count):
-        for k in range(count):
-            ids = ios[...] + (slot0 + 8 * k).astype(I16)
-            hi = [jnp.zeros((8, LANES), BF16)] * 3
-            lo = list(hi)
-            for a in range(8):
-                m = cs[a] == ids
-                for j in range(3):
-                    hi[j] = jnp.where(m, ghs[j * 8 + a], hi[j])
-                    lo[j] = jnp.where(m, gls[j * 8 + a], lo[j])
-            r = pl.ds(row0 + 8 * k, 8)
+    for t in range(chunks):
+        e0 = t * LANES
+        for a in range(8):
+            cs[t, a] = jnp.broadcast_to(conn_s[a : a + 1, e0 : e0 + LANES], (8, LANES)).astype(I16)
             for j in range(3):
-                hi_ref[t, r, j * LANES : (j + 1) * LANES] = hi[j]
-                lo_ref[t, r, j * LANES : (j + 1) * LANES] = lo[j]
-
-    unit = 8
-
-    def chunk(t, carry):
-        e0 = pl.multiple_of(t * LANES, LANES)
+                g = jnp.broadcast_to(grad_s[j, a : a + 1, e0 : e0 + LANES], (8, LANES))
+                hi, lo = split(g)
+                ghs[t, j * 8 + a] = hi
+                gls[t, j * 8 + a] = lo
+
+    def unit(hi_ref, lo_ref, t, row0, slot0):
+        ids = ios[...] + slot0.astype(I16)
+        hi = [jnp.zeros((8, LANES), BF16)] * 3
+        lo = list(hi)
         for a in range(8):
-            cs[a] = jnp.broadcast_to(conn_s[a : a + 1, pl.ds(e0, LANES)], (8, LANES)).astype(I16)
+            m = cs[t, a] == ids
             for j in range(3):
-                g = jnp.broadcast_to(grad_s[j, a : a + 1, pl.ds(e0, LANES)], (8, LANES))
-                hi, lo = split(g)
-                ghs[j * 8 + a] = hi
-                gls[j * 8 + a] = lo
-
-        def own_rows(s, carry):
-            s0 = pl.multiple_of(s * (8 * unit), 8 * unit)
-            units(wh_ref, wl_ref, t, s0, s0, unit)
+                hi[j] = jnp.where(m, ghs[t, j * 8 + a], hi[j])
+                lo[j] = jnp.where(m, gls[t, j * 8 + a], lo[j])
+        r = pl.ds(row0, 8)
+        for j in range(3):
+            hi_ref[r, j * LANES : (j + 1) * LANES] = hi[j]
+            lo_ref[r, j * LANES : (j + 1) * LANES] = lo[j]
+
+    own_units = 16
+    for t in range(chunks):
+
+        def own_rows(s, carry, t=t):
+            row0 = pl.multiple_of(s * (8 * own_units), 8 * own_units)
+            for u in range(own_units):
+                unit(wh[t], wl[t], t, row0 + 8 * u, row0 + 8 * u)
             return carry
 
-        lax.fori_loop(0, node_total // (8 * unit), own_rows, 0)
-
-        def halo_rows(j, carry):
-            col = pl.ds(pl.multiple_of(j * LANES, LANES), LANES)
-            part = dot(phi_ref[...], wh_ref[t, :, col], NN)
-            own_ref[t, :, col] = part[:half] + part[half:] + dot(phi_ref[0:half], wl_ref[t, :, col], NN)
-            for k in range(runs_each):
-                run = j * runs_each + k
-                row0 = pl.multiple_of(run * sec_width, sec_width)
-                units(vh_ref, vl_ref, t, row0, bases[run], sec_width // 8)
-            return carry
-
-        lax.fori_loop(0, 3, halo_rows, 0)
-        return carry
-
-    lax.fori_loop(0, chunks, chunk, 0)
-
-
-def element_kernel(amps_ref, lame_ref, own_ref, a_ref, b_ref, c_ref, d_ref, vh_ref, vl_ref,
-                   pio_ref, modal_ref, hal, disp, grad_h, grad_l):
-    chunks = vh_ref.shape[0]
+        lax.fori_loop(0, node_total // (8 * own_units), own_rows, 0)
+        jobs = [(k, u) for k in range(run) for u in range(stretch // 8)]
+        pieces = [(j, k, low) for j in range(3) for k in range(node_total // LANES) for low in (False, True)]
+        done = 0
+        for p, (j, k, low) in enumerate(pieces):
+            col = slice(j * LANES, (j + 1) * LANES)
+            rows = slice(k * LANES, (k + 1) * LANES)
+            if low:
+                part = dot(phi_s[0:half, rows], wl[t][rows, col], NN)
+            else:
+                part = dot(phi_s[:, rows], wh[t][rows, col], NN)
+                part = part[:half] + part[half:]
+            upto = len(jobs) * (p + 1) // len(pieces)
+            for q, u in jobs[done:upto]:
+                unit(vh[t], vl[t], t, q * stretch + 8 * u, bases[q] + 8 * u)
+            done = upto
+            if k == 0 and not low:
+                own_ref[t, :, col] = part
+            else:
+                own_ref[t, :, col] += part
+
+
+def element_kernel(amps_ref, lame_ref, own_ref, a_ref, b_ref, c_ref, d_ref, *refs, scale):
+    chunks = own_ref.shape[0]
+    vh, vl = refs[:chunks], refs[chunks : 2 * chunks]
+    pio_ref, modal_ref, hal, disp, grad_h, grad_l = refs[2 * chunks :]
     modes, combos = amps_ref.shape
     half = 3 * modes
     col = 0
@@ -193,8 +203,8 @@
     amp = jnp.concatenate([amp_h, amp_h, amp_l], axis=1)
 
     def gradient(t):
-        part = dot(hal[...], vh_ref[t], NN)
-        grad = own_ref[t] + part[:half] + part[half:] + dot(hal[0:half], vl_ref[t], NN)
+        part = dot(hal[...], vh[t][...], NN)
+        grad = own_ref[t] + part[:half] + part[half:] + dot(hal[0:half], vl[t][...], NN)
         gh, gl = split(grad)
         grad_h[t] = gh
         grad_l[t] = gl
@@ -244,46 +254,59 @@
             gradient(t + 1)
         stress(t)
         acc = project(t, acc)
-    modal_ref[...] = acc
-
-
-def force_rows(pio_ref, wh_ref, wl_ref, t):
+    modal_ref[...] = acc * scale
+
+
+def force_rows(pio_ref, wh, wl, t):
     half = pio_ref.shape[1] // 2
-    part = dot(pio_ref[t], wh_ref[t], NT)
-    return part[:half] + part[half:] + dot(pio_ref[t, 0:half, :], wl_ref[t], NT)
-
-
-def halo_kernel(pio_ref, wh_ref, wl_ref, after_ref, *out_refs):
+    part = dot(pio_ref[t], wh[t][...], NT)
+    return part[:half] + part[half:] + dot(pio_ref[t, 0:half, :], wl[t][...], NT)
+
+
+def halo_kernel(pio_ref, modal_ref, after_ref, *refs):
     del after_ref
-    chunks = wh_ref.shape[0]
-    for o in out_refs:
-        o[...] = jnp.zeros_like(o)
-
-    def chunk(t, carry):
-        part = force_rows(pio_ref, wh_ref, wl_ref, t)
+    chunks, rows, _ = pio_ref.shape
+    rows //= 2
+    wh, wl, out_refs = refs[:chunks], refs[chunks : 2 * chunks], refs[2 * chunks :]
+    for t in range(chunks):
+        part = force_rows(pio_ref, wh, wl, t)
         col = 0
         for o in out_refs:
-            o[...] += part[:, col : col + o.shape[1]]
+            piece = part[:, col : col + o.shape[1]]
+            o[0:rows, :] = piece if t == 0 else o[0:rows, :] + piece
             col += o.shape[1]
-        return carry
-
-    lax.fori_loop(0, chunks, chunk, 0)
-
-
-def sum_kernel(a_ref, b_ref, after_ref, out_ref):
+    out_refs[2][rows:, 0 : modal_ref.shape[1]] = modal_ref[...]
+
+
+def ride_kernel(sent_ref, got_ref, into_ref, out_ref, *, rows, combos):
+    del into_ref
+    out_ref[rows:, 0:combos] = sent_ref[rows:, 0:combos] + got_ref[rows:, 0:combos]
+
+
+def land_kernel(sent_ref, got_ref, *refs, rows):
+    out_ref = refs[-1]
+    combos = out_ref.shape[1]
+    out_ref[...] = sent_ref[rows:, 0:combos] + got_ref[rows:, 0:combos]
+
+
+def sum_kernel(a_ref, b_ref, *refs):
+    out_ref = refs[-1]
+    out_ref[...] = a_ref[...] + b_ref[...]
+
+
+def own_kernel(pio_ref, after_ref, *refs, first):
     del after_ref
-    out_ref[...] = a_ref[...] + b_ref[...]
-
-
-def own_kernel(pio_ref, wh_ref, wl_ref, after_ref, out_ref):
-    del after_ref
-    out_ref[...] = jnp.zeros_like(out_ref)
-
-    def chunk(t, carry):
-        out_ref[...] += force_rows(pio_ref, wh_ref, wl_ref, t)
-        return carry
-
-    lax.fori_loop(0, wh_ref.shape[0], chunk, 0)
+    *before, out_ref = refs
+    chunks = (len(before) - (first > 0)) // 2
+    wh, wl = before[:chunks], before[chunks : 2 * chunks]
+    for k in range(chunks):
+        half = pio_ref.shape[1] // 2
+        part = dot(pio_ref[first + k], wh[k][...], NT)
+        part = part[:half] + part[half:] + dot(pio_ref[first + k, 0:half, :], wl[k][...], NT)
+        if k == 0:
+            out_ref[...] = part + before[-1][...] if first else part
+        else:
+            out_ref[...] += part
 
 
 def add_kernel(own_ref, hot_ref, a_ref, b_ref, c_ref, d_ref, out_hbm, back, out_s, sems):
@@ -292,7 +315,7 @@
     combos = rows // 3
     col = 0
     for r in (a_ref, b_ref, c_ref, d_ref):
-        hi, lo = split(r[...])
+        hi, lo = split(r[0:rows, :])
         back[0:rows, col : col + r.shape[1]] = hi
         back[rows:, col : col + r.shape[1]] = lo
         col += r.shape[1]
@@ -311,7 +334,7 @@
         c.wait()
 
 
-def call(kernel, out_shape, args, scratch=(), vmem=24, hbm_in=(), any_in=(), any_out=False, flops=0):
+def call(kernel, out_shape, args, scratch=(), vmem=24, hbm_in=(), any_in=(), any_out=False, flops=0, alias=None):
     vm = pl.BlockSpec(memory_space=pltpu.VMEM)
     hbm = pl.BlockSpec(memory_space=pltpu.HBM)
     anywhere = pl.BlockSpec(memory_space=pl.ANY)
@@ -324,6 +347,7 @@
         in_specs=[hbm if i in hbm_in else anywhere if i in any_in else vm for i in range(len(args))],
         out_specs=[out] * len(out_shape) if many else out,
         scratch_shapes=list(scratch),
+        input_output_aliases=alias or {},
         compiler_params=pltpu.CompilerParams(vmem_limit_bytes=vmem * MIB),
         cost_estimate=pl.CostEstimate(flops=flops, bytes_accessed=1 << 20, transcendentals=0),
     )(*args)
@@ -370,27 +394,29 @@
         hbm_in=range(6),
     )
     halo = exchange(*packets)
-    wh, wl, vh, vl, own_grad = call(
-        functools.partial(build_kernel, dom_width=dom_width, sec_width=sec_width),
-        [sds((chunks, node_total, cols), BF16)] * 2
-        + [sds((chunks, halo_width, cols), BF16)] * 2
+    *elem, own_grad = call(
+        functools.partial(build_kernel, dom_width=dom_width, sec_width=sec_width, chunks=chunks),
+        [sds((node_total, cols), BF16)] * (2 * chunks)
+        + [sds((halo_width, cols), BF16)] * (2 * chunks)
         + [sds((chunks, 3 * modes, cols), F32)],
         (phi, conn_v, grads_v),
         scratch=[
             pltpu.VMEM((8, elems), jnp.int32),
             pltpu.VMEM((3, 8, elems), F32),
-            pltpu.VMEM((8, 8, LANES), I16),
-            pltpu.VMEM((24, 8, LANES), BF16),
-            pltpu.VMEM((24, 8, LANES), BF16),
+            pltpu.VMEM((chunks, 8, 8, LANES), I16),
+            pltpu.VMEM((chunks, 24, 8, LANES), BF16),
+            pltpu.VMEM((chunks, 24, 8, LANES), BF16),
             pltpu.VMEM((8, LANES), I16),
-            pltpu.SMEM((halo_width // sec_width,), jnp.int32),
+            pltpu.VMEM((6 * modes, node_total), BF16),
+            pltpu.SMEM((2 * halo_width // sec_width,), jnp.int32),
         ],
         flops=6 * 3 * modes * node_total * 3 * elems,
     )
+    all_nodes = node_total * lax.axis_size("sector") * lax.axis_size("dom")
     pio, modal = call(
-        element_kernel,
+        functools.partial(element_kernel, scale=1.0 / math.sqrt(3.0 * all_nodes)),
         [sds((chunks, 6 * combos, cols), BF16), sds((modes, combos), F32)],
-        (amplitudes.T, lame_v, own_grad, *halo, vh, vl),
+        (amplitudes.T, lame_v, own_grad, *halo, *elem[2 * chunks :]),
         scratch=[
             pltpu.VMEM((6 * modes, halo_width), BF16),
             pltpu.VMEM((chunks, 3, combos, cols), F32),
@@ -398,35 +424,67 @@
             pltpu.VMEM((chunks, 3 * modes, cols), BF16),
         ],
     )
-    steps = []
-    for axis in ("sector", "dom"):
-        count = lax.axis_size(axis)
-        step = 1
-        while step < count:
-            steps.append((axis, [(i, i ^ step) for i in range(count)]))
-            step *= 2
-
-    def other(x, k):
-        return lax.ppermute(x, *steps[k])
-
-    modal = modal + other(modal, 0)
-    across = other(modal, 1)
-    back = call(
+    rows = 3 * combos
+    sector, dom = lax.axis_size("sector"), lax.axis_size("dom")
+
+    def other(x, axis, step):
+        return lax.ppermute(x, axis, [(i, i ^ step) for i in range(lax.axis_size(axis))])
+
+    def fold(x, axis, step, *after, hbm_in=()):
+        args = (x, other(x, axis, step), *after)
+        anywhere = [i for i in range(2, len(args)) if i not in hbm_in]
+        return call(sum_kernel, sds(x.shape, F32), args, any_in=anywhere, hbm_in=hbm_in)
+
+    def scatter_own(first, last, after, before=()):
+        return call(
+            functools.partial(own_kernel, first=first),
+            sds((rows, node_total), F32),
+            (pio, after, *elem[first:last], *elem[chunks + first : chunks + last], *before),
+            any_in=(1,),
+            flops=2 * 3 * rows * node_total * 3 * LANES * (last - first),
+        )
+
+    own = scatter_own(0, 1, modal)
+    modal = fold(modal, "dom", 1, own)
+    ride = sector == 4
+    heights = (rows, rows, rows + modes, rows + modes if ride else rows)
+    back_a, back_b, back_c, back_d = call(
         halo_kernel,
-        [sds((3 * combos, w), F32) for w in widths],
-        (pio, vh, vl, modal),
-        any_in=(3,),
-    )
-    modal = call(sum_kernel, sds(modal.shape, F32), (modal, across, back[3]), any_in=(2,))
-    modal = modal + other(modal, 2)
-    returned = exchange(*back)
-    own = call(
-        own_kernel,
-        sds((3 * combos, node_total), F32),
-        (pio, wh, wl, modal),
-        any_in=(3,),
-        flops=6 * 3 * combos * node_total * 3 * elems,
-    )
+        [sds((h, w), F32) for h, w in zip(heights, widths)],
+        (pio, modal, own, *elem[2 * chunks :]),
+        any_in=(2,),
+    )
+    got_c = swap(back_c, "sector", True, True)
+    got_a = swap(back_a, "dom", True, False)
+    if ride:
+        back_d = call(
+            functools.partial(ride_kernel, rows=rows, combos=combos),
+            sds(back_d.shape, F32),
+            (back_c, got_c, back_d),
+            any_in=(2,),
+            alias={2: 0},
+        )
+    got_d = swap(back_d, "sector", False, True)
+    back_b = call(hold_kernel, sds(back_b.shape, F32), (back_b, back_d), any_in=(0, 1), any_out=True, alias={0: 0})
+    got_b = swap(back_b, "dom", False, False)
+    own = scatter_own(1, chunks - 1, back_d, (own,))
+    landed = (back_d, got_d) if ride else (back_c, got_c)
+    modal = call(
+        functools.partial(land_kernel, rows=rows),
+        sds(modal.shape, F32),
+        (*landed, own),
+        any_in=(2,),
+    )
+    own = scatter_own(chunks - 1, chunks, modal, (own,))
+    step = 2
+    while not ride and step < sector:
+        modal = modal + other(modal, "sector", step)
+        step *= 2
+    step = 2
+    while 4 * step <= dom:
+        modal = fold(modal, "dom", step, own)
+        step *= 2
+    returned = (got_a, got_b, got_c, got_d)
     forces = call(
         add_kernel,
         sds((3, combos, node_total), F32),
@@ -438,10 +496,8 @@
         ],
         any_out=True,
     )
-    for k in range(3, len(steps)):
-        modal = modal + other(modal, k)
-    all_nodes = node_total * lax.axis_size("sector") * lax.axis_size("dom")
-    return forces.transpose(1, 0, 2), modal.T / math.sqrt(3.0 * all_nodes)
+    modal = fold(modal, "dom", dom // 2, forces, hbm_in=(2,))
+    return forces.transpose(1, 0, 2), modal.T
 
 
 def solution(mesh):

time: 54 us -> 51.8 us (0.959)
  Pallas kernels: 30.3 us -> 28.3 us
  waiting for transfers between devices: 3.37 us -> 5.14 us
  starting transfers between devices: 18.7 us -> 17.4 us
  other arithmetic: 0.63 us -> 0 us
    pallas_call x7 -> x14, Pallas kernels: 30.3 us -> 28.3 us  [call(): pl.pallas_call(kernel, out_shape=out_shape, in_specs=[hbm if i in hbm_in...]
    ppermute x8, waiting for transfers between devices: 0.02 us -> 1.95 us  [swap(): return lax.ppermute(x, axis, [(i, j % count) for i, j in pairs])]
    ppermute x8, starting transfers between devices: 9.65 us -> 8.48 us  [swap(): return lax.ppermute(x, axis, [(i, j % count) for i, j in pairs])]
    div x1 -> x0, other arithmetic: 0.61 us -> none  [local(): return (forces.transpose(1, 0, 2), modal.T / math.sqrt(3.0 * all_nodes))]
    ppermute x5 -> x3, waiting for transfers between devices: 3.35 us -> 3.19 us  [other(): lax.ppermute(x, axis, [(i, i ^ step) for i in range(lax.axis_size(axis))])]
    ppermute x5 -> x3, starting transfers between devices: 9.06 us -> 8.92 us  [other(): lax.ppermute(x, axis, [(i, i ^ step) for i in range(lax.axis_size(axis))])]
  transfers between devices with their start and end apart: 13 -> 11, of which waited for: 3 -> 4; matrix products, arithmetic and copies ran while one was open for 1% -> 0% of each run, Pallas kernels for 40% -> 33%
where the time goes in v3:
time: 51.8 us; the launch traced here: 51.6 us
  Pallas kernels  28.3 us (55%)
  starting transfers between devices  17.4 us (34%)
  waiting for transfers between devices  5.14 us (10%)
  between operations  0.76 us (1%)
    pallas_call x14, Pallas kernels, call(): pl.pallas_call(kernel, out_shape=out_shape, in_specs=[hbm if i in hbm_in...  28.3 us
    ppermute x3, starting transfers between devices, other(): lax.ppermute(x, axis, [(i, i ^ step) for i in range(lax.axis_size(axis))])  8.92 us
    ppermute x8, starting transfers between devices, swap(): return lax.ppermute(x, axis, [(i, j % count) for i, j in pairs])  8.48 us
    ppermute x3, waiting for transfers between devices, other(): lax.ppermute(x, axis, [(i, i ^ step) for i in range(lax.axis_size(axis))])  3.19 us
    ppermute x8, waiting for transfers between devices, swap(): return lax.ppermute(x, axis, [(i, j % count) for i, j in pairs])  1.95 us
  transfers between devices with their start and end apart: 11, of which 4 were waited for; matrix products, arithmetic and copies ran while one was open for 0% of the time, Pallas kernels for 33%

profile of v3, /device:TPU:0, one launch (start us, length us, event | category | flops | bytes accessed | tf_op | source)
XLA Modules:
  0.0 51.6 jit_solution(15207761354505211651)
XLA Ops:
  0.6 1.9 %shard_map.86 = (f32[144,256]{1,0:T(8,128)S(1)}, f32[144,256]{1,0:T(8,128)S(1)}, f32[144,128]{1,0:T(8,128)S(1)}, f32[144,128]{1,0:T(8,128)S(1)}, bf16[1024,768]{...) custom-call(f32[3,48,1024]{2,1,0:T(8,128)} %bitcast.7, ...), custom_call_target="tpu_custom_call" | custom-call | bytes 1048576 | tf_op jit(solution)/shard_map/pallas_call | solution.py:344
  2.6 0.5 %collective-permute-start.2 = (f32[144,128]{1,0:T(8,128)S(1)}, f32[144,128]{1,0:T(8,128)S(1)}, u32[]{:S(2)}, u32[]{:S(2)}) collective-permute-start(f32[144,128]{1,0:T(8,128)S(1)} %get-tuple-element.41), channel_id=1, source_target_pairs={{0,8},{8,0},{16,24},{24,16},{1,9},{9,1},{17,25},{25,17},{2,10},{10... | collective-permute-start | bytes 221192 | tf_op jit(solution)/shard_map/ppermute | solution.py:40
  3.1 2.6 %collective-permute-start.3 = (f32[144,128]{1,0:T(8,128)S(1)}, f32[144,128]{1,0:T(8,128)S(1)}, u32[]{:S(2)}, u32[]{:S(2)}) collective-permute-start(f32[144,128]{1,0:T(8,128)S(1)} %get-tuple-element.42), channel_id=1, source_target_pairs={{0,24},{8,16},{16,8},{24,0},{1,25},{9,17},{17,9},{25,1},{2,26},{10... | collective-permute-start | bytes 221192 | tf_op jit(solution)/shard_map/ppermute | solution.py:40
  5.7 1.5 %collective-permute-start = (f32[144,256]{1,0:T(8,128)S(1)}, f32[144,256]{1,0:T(8,128)S(1)}, u32[]{:S(2)}, u32[]{:S(2)}) collective-permute-start(f32[144,256]{1,0:T(8,128)S(1)} %get-tuple-element.39), channel_id=1, source_target_pairs={{0,1},{1,0},{2,3},{3,2},{4,5},{5,4},{6,7},{7,6},{8,9},{9,8},{10,11... | collective-permute-start | bytes 442376 | tf_op jit(solution)/shard_map/ppermute | solution.py:40
  7.2 0.7 %collective-permute-start.1 = (f32[144,256]{1,0:T(8,128)S(1)}, f32[144,256]{1,0:T(8,128)S(1)}, u32[]{:S(2)}, u32[]{:S(2)}) collective-permute-start(f32[144,256]{1,0:T(8,128)S(1)} %get-tuple-element.40), channel_id=1, source_target_pairs={{1,2},{2,1},{3,4},{4,3},{5,6},{6,5},{9,10},{10,9},{11,12},{12,11},... | collective-permute-start | bytes 442376 | tf_op jit(solution)/shard_map/ppermute | solution.py:40
  7.9 0.0 copy-start
  7.9 10.7 %shard_map.87 = (bf16[1024,768]{1,0:T(8,128)(2,1)S(1)}, bf16[1024,768]{1,0:T(8,128)(2,1)S(1)}, bf16[1024,768]{1,0:T(8,128)(2,1)S(1)}, bf16[1024,768]{1,0:T(8,128...) custom-call(bf16[288,1024]{1,0:T(8,128)(2,1)S(1)} %get-tuple-element, ...), custom_call_target="tpu_custom_call" | custom-call | flops 2717908992 | bytes 1048576 | tf_op jit(solution)/shard_map/pallas_call | solution.py:344
  18.6 0.0 collective-permute-done.2.c_ref
  18.6 0.0 collective-permute-done.3.d_ref
  18.6 0.0 collective-permute-done.a_ref
  18.6 0.0 collective-permute-done.1.b_ref
  18.6 0.0 copy-done
  18.6 5.1 %shard_map.88 = (bf16[4,384,768]{2,1,0:T(8,128)(2,1)S(1)}, f32[48,64]{1,0:T(8,128)S(1)}) custom-call(f32[48,64]{1,0:T(8,128)S(1)} %bitcast.5, f32[2,1024]{1,0:T(2,128)S(1)} %get-tuple-element.34.lame_ref, f32[4,144,768]{2,1,0:T(8,128)S(1)} %get-tuple-element.38.own_ref, f32[144,256]{1,0:T(8,128)S(1)} %collective-permute-done.a_ref, ...), custom_call_target="tpu_custom_call" | custom-call | bytes 1048576 | tf_op jit(solution)/shard_map/pallas_call | solution.py:344
  23.8 4.3 %collective-permute-start.4 = (f32[48,64]{1,0:T(8,128)S(1)}, f32[48,64]{1,0:T(8,128)S(1)}, u32[]{:S(2)}, u32[]{:S(2)}) collective-permute-start(f32[48,64]{1,0:T(8,128)S(1)} %get-tuple-element.52.after_ref.a_ref), channel_id=1, source_target_pairs={{0,1},{1,0},{2,3},{3,2},{4,5},{5,4},{6,7},{7,6},{8,9},{9,8},{10,11... | collective-permute-start | bytes 36872 | tf_op jit(solution)/shard_map/ppermute | solution.py:431
  28.1 1.3 %shard_map.89.refs_0_.after_ref.refs_4_ = f32[192,1024]{1,0:T(8,128)S(1)} custom-call(bf16[4,384,768]{2,1,0:T(8,128)(2,1)S(1)} %get-tuple-element.51.pio_ref, f32[48,64]{1,0:T(8,128)S(1)} %get-tuple-element.52.after_ref.a_ref, bf16[1024,768]{1,0:T(8,128)(2,1)S(1)} %get-tuple-element.53.refs_0_, bf16[1024,768]{1,0:T(8,128)(2,1)S(1)} %get-tuple-element.54.refs_1_), custom_call_target="tpu_custom_call" | custom-call | flops 905969664 | bytes 1048576 | tf_op jit(solution)/shard_map/pallas_call | solution.py:344
  29.4 0.5 %collective-permute-done.4.b_ref = f32[48,64]{1,0:T(8,128)S(1)} collective-permute-done((f32[48,64]{1,0:T(8,128)S(1)}, f32[48,64]{1,0:T(8,128)S(1)}, u32[]{:S(2)}, u32[]{:S(2)}) %collective-permute-start.4) | collective-permute-done | bytes 12320 | tf_op jit(solution)/shard_map/ppermute | solution.py:431
  29.9 3.4 %shard_map.91 = (f32[192,256]{1,0:T(8,128)S(1)}, f32[192,256]{1,0:T(8,128)S(1)}, f32[240,128]{1,0:T(8,128)S(1)}, f32[240,128]{1,0:T(8,128)S(1)}) custom-call(bf16[4,384,768]{2,1,0:T(8,128)(2,1)S(1)} %get-tuple-element.51.pio_ref, f32[48,64]{1,0:T(8,128)S(1)} %shard_map.90.modal_ref, f32[192,1024]{1,0:T(8,128)S(1)} %shard_map.89.refs_0_.after_ref.refs_4_, ...), custom_call_target="tpu_custom_call" | custom-call | bytes 1048576 | tf_op jit(solution)/shard_map/pallas_call | solution.py:344
  33.3 0.1 collective-permute-start.5
  33.4 2.1 %collective-permute-start.7 = (f32[192,256]{1,0:T(8,128)S(1)}, f32[192,256]{1,0:T(8,128)S(1)}, u32[]{:S(2)}, u32[]{:S(2)}) collective-permute-start(f32[192,256]{1,0:T(8,128)S(1)} %get-tuple-element.64), channel_id=1, source_target_pairs={{0,1},{1,0},{2,3},{3,2},{4,5},{5,4},{6,7},{7,6},{8,9},{9,8},{10,11... | collective-permute-start | bytes 589832 | tf_op jit(solution)/shard_map/ppermute | solution.py:40
  35.5 0.0 collective-permute-done.5.got_ref.c_ref
  35.5 0.3 collective-permute-start.6
  35.8 0.7 %collective-permute-start.8 = (f32[192,256]{1,0:T(8,128)S(1)}, f32[192,256]{1,0:T(8,128)S(1)}, u32[]{:S(2)}, u32[]{:S(2)}) collective-permute-start(f32[192,256]{1,0:T(8,128)S(1)} %shard_map.96), channel_id=1, source_target_pairs={{1,2},{2,1},{3,4},{4,3},{5,6},{6,5},{9,10},{10,9},{11,12},{12,11},... | collective-permute-start | bytes 589832 | tf_op jit(solution)/shard_map/ppermute | solution.py:40
  36.5 2.4 %shard_map.93.refs_0_.refs_2_ = f32[192,1024]{1,0:T(8,128)S(1)} custom-call(bf16[4,384,768]{2,1,0:T(8,128)(2,1)S(1)} %get-tuple-element.51.pio_ref, f32[240,128]{1,0:T(8,128)S(1)} %shard_map.92.after_ref.sent_ref, bf16[1024,768]{1,0:T(8,128)(2,1)S(1)} %get-tuple-element.57.refs_0_, bf16[1024,768]{1,0:T(8,128)(2,1)S(1)} %get-tuple-element.58.refs_1_, ...), custom_call_target="tpu_custom_call" | custom-call | flops 1811939328 | bytes 1048576 | tf_op jit(solution)/shard_map/pallas_call | solution.py:344
  38.9 1.9 %collective-permute-done.6.got_ref.d_ref = f32[240,128]{1,0:T(8,128)S(1)} collective-permute-done((f32[240,128]{1,0:T(8,128)S(1)}, f32[240,128]{1,0:T(8,128)S(1)}, u32[]{:S(2)}, u32[]{:S(2)}) %collective-permute-start.6) | collective-permute-done | bytes 122912 | tf_op jit(solution)/shard_map/ppermute | solution.py:40
  40.8 2.0 %collective-permute-start.9 = (f32[48,64]{1,0:T(8,128)S(1)}, f32[48,64]{1,0:T(8,128)S(1)}, u32[]{:S(2)}, u32[]{:S(2)}) collective-permute-start(f32[48,64]{1,0:T(8,128)S(1)} %shard_map.94.after_ref.a_ref), channel_id=1, source_target_pairs={{0,2},{1,3},{2,0},{3,1},{4,6},{5,7},{6,4},{7,5},{8,10},{9,11},{10,... | collective-permute-start | bytes 36872 | tf_op jit(solution)/shard_map/ppermute | solution.py:431
  42.8 1.3 %shard_map.95.own_ref.refs_0_ = f32[192,1024]{1,0:T(8,128)S(1)} custom-call(bf16[4,384,768]{2,1,0:T(8,128)(2,1)S(1)} %get-tuple-element.51.pio_ref, f32[48,64]{1,0:T(8,128)S(1)} %shard_map.94.after_ref.a_ref, bf16[1024,768]{1,0:T(8,128)(2,1)S(1)} %get-tuple-element.61.refs_0_, bf16[1024,768]{1,0:T(8,128)(2,1)S(1)} %get-tuple-element.62.refs_1_, ...), custom_call_target="tpu_custom_call" | custom-call | flops 905969664 | bytes 1048576 | tf_op jit(solution)/shard_map/pallas_call | solution.py:344
  44.1 1.9 %collective-permute-done.9.b_ref = f32[48,64]{1,0:T(8,128)S(1)} collective-permute-done((f32[48,64]{1,0:T(8,128)S(1)}, f32[48,64]{1,0:T(8,128)S(1)}, u32[]{:S(2)}, u32[]{:S(2)}) %collective-permute-start.9) | collective-permute-done | bytes 12320 | tf_op jit(solution)/shard_map/ppermute | solution.py:431
  46.0 2.6 %collective-permute-start.10 = (f32[48,64]{1,0:T(8,128)S(1)}, f32[48,64]{1,0:T(8,128)S(1)}, u32[]{:S(2)}, u32[]{:S(2)}) collective-permute-start(f32[48,64]{1,0:T(8,128)S(1)} %shard_map.98.a_ref), channel_id=1, source_target_pairs={{0,4},{1,5},{2,6},{3,7},{4,0},{5,1},{6,2},{7,3},{8,12},{9,13},{10,... | collective-permute-start | bytes 36872 | tf_op jit(solution)/shard_map/ppermute | solution.py:431
  48.6 0.0 collective-permute-done.7.a_ref
  48.6 0.0 collective-permute-done.8.b_ref
  48.6 1.6 %shard_map.97.refs_0_ = f32[3,64,1024]{2,1,0:T(8,128)} custom-call(f32[192,1024]{1,0:T(8,128)S(1)} %shard_map.95.own_ref.refs_0_, bf16[1024,768]{1,0:T(8,128)(2,1)S(1)} %get-tuple-element.63.hot_ref, f32[192,256]{1,0:T(8,128)S(1)} %collective-permute-done.7.a_ref, f32[192,256]{1,0:T(8,128)S(1)} %collective-permute-done.8.b_ref, ...), custom_call_target="tpu_custom_call" | custom-call | bytes 1048576 | tf_op jit(solution)/shard_map/pallas_call | solution.py:344
  50.2 0.8 %collective-permute-done.10.b_ref = f32[48,64]{1,0:T(8,128)S(1)} collective-permute-done((f32[48,64]{1,0:T(8,128)S(1)}, f32[48,64]{1,0:T(8,128)S(1)}, u32[]{:S(2)}, u32[]{:S(2)}) %collective-permute-start.10) | collective-permute-done | bytes 12320 | tf_op jit(solution)/shard_map/ppermute | solution.py:431
  51.0 0.6 %shard_map.99 = f32[48,64]{1,0:T(8,128)} custom-call(f32[48,64]{1,0:T(8,128)S(1)} %shard_map.98.a_ref, f32[48,64]{1,0:T(8,128)S(1)} %collective-permute-done.10.b_ref, f32[3,64,1024]{2,1,0:T(8,128)} %shard_map.97.refs_0_), custom_call_target="tpu_custom_call" | custom-call | bytes 1048576 | tf_op jit(solution)/shard_map/pallas_call | solution.py:344
  (5 shorter events, 0.0 us)
Async XLA Ops:
  2.6 16.0 %collective-permute-start.2 = (f32[144,128]{1,0:T(8,128)S(1)}, f32[144,128]{1,0:T(8,128)S(1)}, u32[]{:S(2)}, u32[]{:S(2)}) collective-permute-start(f32[144,128]{1,0:T(8,128)S(1)} %get-tuple-element.41), channel_id=1, source_target_pairs={{0,8},{8,0},{16,24},{24,16},{1,9},{9,1},{17,25},{25,17},{2,10},{10... | collective-permute-start | bytes 221192 | tf_op jit(solution)/shard_map/ppermute | solution.py:40
  3.1 15.5 %collective-permute-start.3 = (f32[144,128]{1,0:T(8,128)S(1)}, f32[144,128]{1,0:T(8,128)S(1)}, u32[]{:S(2)}, u32[]{:S(2)}) collective-permute-start(f32[144,128]{1,0:T(8,128)S(1)} %get-tuple-element.42), channel_id=1, source_target_pairs={{0,24},{8,16},{16,8},{24,0},{1,25},{9,17},{17,9},{25,1},{2,26},{10... | collective-permute-start | bytes 221192 | tf_op jit(solution)/shard_map/ppermute | solution.py:40
  5.7 12.9 %collective-permute-start = (f32[144,256]{1,0:T(8,128)S(1)}, f32[144,256]{1,0:T(8,128)S(1)}, u32[]{:S(2)}, u32[]{:S(2)}) collective-permute-start(f32[144,256]{1,0:T(8,128)S(1)} %get-tuple-element.39), channel_id=1, source_target_pairs={{0,1},{1,0},{2,3},{3,2},{4,5},{5,4},{6,7},{7,6},{8,9},{9,8},{10,11... | collective-permute-start | bytes 442376 | tf_op jit(solution)/shard_map/ppermute | solution.py:40
  7.2 11.4 %collective-permute-start.1 = (f32[144,256]{1,0:T(8,128)S(1)}, f32[144,256]{1,0:T(8,128)S(1)}, u32[]{:S(2)}, u32[]{:S(2)}) collective-permute-start(f32[144,256]{1,0:T(8,128)S(1)} %get-tuple-element.40), channel_id=1, source_target_pairs={{1,2},{2,1},{3,4},{4,3},{5,6},{6,5},{9,10},{10,9},{11,12},{12,11},... | collective-permute-start | bytes 442376 | tf_op jit(solution)/shard_map/ppermute | solution.py:40
  7.9 10.7 %copy-start = (f32[64,48]{0,1:T(8,128)S(1)}, f32[64,48]{0,1:T(8,128)}, u32[]{:S(2)}) copy-start(f32[64,48]{0,1:T(8,128)} %param.7) | copy-start | bytes 36868
  23.8 6.1 %collective-permute-start.4 = (f32[48,64]{1,0:T(8,128)S(1)}, f32[48,64]{1,0:T(8,128)S(1)}, u32[]{:S(2)}, u32[]{:S(2)}) collective-permute-start(f32[48,64]{1,0:T(8,128)S(1)} %get-tuple-element.52.after_ref.a_ref), channel_id=1, source_target_pairs={{0,1},{1,0},{2,3},{3,2},{4,5},{5,4},{6,7},{7,6},{8,9},{9,8},{10,11... | collective-permute-start | bytes 36872 | tf_op jit(solution)/shard_map/ppermute | solution.py:431
  33.3 2.2 %collective-permute-start.5 = (f32[240,128]{1,0:T(8,128)S(1)}, f32[240,128]{1,0:T(8,128)S(1)}, u32[]{:S(2)}, u32[]{:S(2)}) collective-permute-start(f32[240,128]{1,0:T(8,128)S(1)} %get-tuple-element.55.sent_ref), channel_id=1, source_target_pairs={{0,8},{8,0},{16,24},{24,16},{1,9},{9,1},{17,25},{25,17},{2,10},{10... | collective-permute-start | bytes 368648 | tf_op jit(solution)/shard_map/ppermute | solution.py:40
  33.4 15.2 %collective-permute-start.7 = (f32[192,256]{1,0:T(8,128)S(1)}, f32[192,256]{1,0:T(8,128)S(1)}, u32[]{:S(2)}, u32[]{:S(2)}) collective-permute-start(f32[192,256]{1,0:T(8,128)S(1)} %get-tuple-element.64), channel_id=1, source_target_pairs={{0,1},{1,0},{2,3},{3,2},{4,5},{5,4},{6,7},{7,6},{8,9},{9,8},{10,11... | collective-permute-start | bytes 589832 | tf_op jit(solution)/shard_map/ppermute | solution.py:40
  35.5 5.3 %collective-permute-start.6 = (f32[240,128]{1,0:T(8,128)S(1)}, f32[240,128]{1,0:T(8,128)S(1)}, u32[]{:S(2)}, u32[]{:S(2)}) collective-permute-start(f32[240,128]{1,0:T(8,128)S(1)} %shard_map.92.after_ref.sent_ref), channel_id=1, source_target_pairs={{0,24},{8,16},{16,8},{24,0},{1,25},{9,17},{17,9},{25,1},{2,26},{10... | collective-permute-start | bytes 368648 | tf_op jit(solution)/shard_map/ppermute | solution.py:40
  35.8 12.8 %collective-permute-start.8 = (f32[192,256]{1,0:T(8,128)S(1)}, f32[192,256]{1,0:T(8,128)S(1)}, u32[]{:S(2)}, u32[]{:S(2)}) collective-permute-start(f32[192,256]{1,0:T(8,128)S(1)} %shard_map.96), channel_id=1, source_target_pairs={{1,2},{2,1},{3,4},{4,3},{5,6},{6,5},{9,10},{10,9},{11,12},{12,11},... | collective-permute-start | bytes 589832 | tf_op jit(solution)/shard_map/ppermute | solution.py:40
  40.8 5.2 %collective-permute-start.9 = (f32[48,64]{1,0:T(8,128)S(1)}, f32[48,64]{1,0:T(8,128)S(1)}, u32[]{:S(2)}, u32[]{:S(2)}) collective-permute-start(f32[48,64]{1,0:T(8,128)S(1)} %shard_map.94.after_ref.a_ref), channel_id=1, source_target_pairs={{0,2},{1,3},{2,0},{3,1},{4,6},{5,7},{6,4},{7,5},{8,10},{9,11},{10,... | collective-permute-start | bytes 36872 | tf_op jit(solution)/shard_map/ppermute | solution.py:431
  46.0 5.0 %collective-permute-start.10 = (f32[48,64]{1,0:T(8,128)S(1)}, f32[48,64]{1,0:T(8,128)S(1)}, u32[]{:S(2)}, u32[]{:S(2)}) collective-permute-start(f32[48,64]{1,0:T(8,128)S(1)} %shard_map.98.a_ref), channel_id=1, source_target_pairs={{0,4},{1,5},{2,6},{3,7},{4,0},{5,1},{6,2},{7,3},{8,12},{9,13},{10,... | collective-permute-start | bytes 36872 | tf_op jit(solution)/shard_map/ppermute | solution.py:431

commit v4 on v3

--- a/solution.py
+++ b/solution.py
@@ -263,8 +263,7 @@
     return part[:half] + part[half:] + dot(pio_ref[t, 0:half, :], wl[t][...], NT)
 
 
-def halo_kernel(pio_ref, modal_ref, after_ref, *refs):
-    del after_ref
+def halo_kernel(pio_ref, *refs):
     chunks, rows, _ = pio_ref.shape
     rows //= 2
     wh, wl, out_refs = refs[:chunks], refs[chunks : 2 * chunks], refs[2 * chunks :]
@@ -275,7 +274,11 @@
             piece = part[:, col : col + o.shape[1]]
             o[0:rows, :] = piece if t == 0 else o[0:rows, :] + piece
             col += o.shape[1]
-    out_refs[2][rows:, 0 : modal_ref.shape[1]] = modal_ref[...]
+
+
+def board_kernel(a_ref, b_ref, into_ref, out_ref, *, rows):
+    del into_ref
+    out_ref[rows:, 0 : a_ref.shape[1]] = a_ref[...] + b_ref[...]
 
 
 def ride_kernel(sent_ref, got_ref, into_ref, out_ref, *, rows, combos):
@@ -444,15 +447,21 @@
             flops=2 * 3 * rows * node_total * 3 * LANES * (last - first),
         )
 
-    own = scatter_own(0, 1, modal)
-    modal = fold(modal, "dom", 1, own)
+    across = other(modal, "dom", 1)
     ride = sector == 4
     heights = (rows, rows, rows + modes, rows + modes if ride else rows)
     back_a, back_b, back_c, back_d = call(
         halo_kernel,
         [sds((h, w), F32) for h, w in zip(heights, widths)],
-        (pio, modal, own, *elem[2 * chunks :]),
+        (pio, *elem[2 * chunks :]),
+        flops=3 * 2 * rows * halo_width * 3 * elems,
+    )
+    back_c = call(
+        functools.partial(board_kernel, rows=rows),
+        sds(back_c.shape, F32),
+        (modal, across, back_c),
         any_in=(2,),
+        alias={2: 0},
     )
     got_c = swap(back_c, "sector", True, True)
     got_a = swap(back_a, "dom", True, False)
@@ -467,7 +476,7 @@
     got_d = swap(back_d, "sector", False, True)
     back_b = call(hold_kernel, sds(back_b.shape, F32), (back_b, back_d), any_in=(0, 1), any_out=True, alias={0: 0})
     got_b = swap(back_b, "dom", False, False)
-    own = scatter_own(1, chunks - 1, back_d, (own,))
+    own = scatter_own(0, chunks // 2, back_d)
     landed = (back_d, got_d) if ride else (back_c, got_c)
     modal = call(
         functools.partial(land_kernel, rows=rows),
@@ -475,7 +484,7 @@
         (*landed, own),
         any_in=(2,),
     )
-    own = scatter_own(chunks - 1, chunks, modal, (own,))
+    own = scatter_own(chunks // 2, chunks, modal, (own,))
     step = 2
     while not ride and step < sector:
         modal = modal + other(modal, "sector", step)

time: 51.8 us -> 48.3 us (0.932)
  starting transfers between devices: 17.4 us -> 15.7 us
  waiting for transfers between devices: 5.14 us -> 3.8 us
    ppermute x3, waiting for transfers between devices: 3.19 us -> 1.09 us  [other(): lax.ppermute(x, axis, [(i, i ^ step) for i in range(lax.axis_size(axis))])]
    ppermute x8, starting transfers between devices: 8.48 us -> 6.91 us  [swap(): return lax.ppermute(x, axis, [(i, j % count) for i, j in pairs])]
    ppermute x8, waiting for transfers between devices: 1.95 us -> 2.7 us  [swap(): return lax.ppermute(x, axis, [(i, j % count) for i, j in pairs])]
    pallas_call x14 -> x13, Pallas kernels: 28.3 us -> 27.9 us  [call(): pl.pallas_call(kernel, out_shape=out_shape, in_specs=[hbm if i in hbm_in...]
  transfers between devices with their start and end apart: 11 -> 11, of which waited for: 4 -> 4; matrix products, arithmetic and copies ran while one was open for 0% -> 0% of each run, Pallas kernels for 33% -> 42%
where the time goes in v4:
time: 48.3 us; the launch traced here: 48.1 us
  Pallas kernels  27.9 us (58%)
  starting transfers between devices  15.7 us (33%)
  waiting for transfers between devices  3.8 us (8%)
  between operations  0.76 us (2%)
    pallas_call x13, Pallas kernels, call(): pl.pallas_call(kernel, out_shape=out_shape, in_specs=[hbm if i in hbm_in...  27.9 us
    ppermute x3, starting transfers between devices, other(): lax.ppermute(x, axis, [(i, i ^ step) for i in range(lax.axis_size(axis))])  8.76 us
    ppermute x8, starting transfers between devices, swap(): return lax.ppermute(x, axis, [(i, j % count) for i, j in pairs])  6.91 us
    ppermute x8, waiting for transfers between devices, swap(): return lax.ppermute(x, axis, [(i, j % count) for i, j in pairs])  2.7 us
    ppermute x3, waiting for transfers between devices, other(): lax.ppermute(x, axis, [(i, i ^ step) for i in range(lax.axis_size(axis))])  1.09 us
  transfers between devices with their start and end apart: 11, of which 4 were waited for; matrix products, arithmetic and copies ran while one was open for 0% of the time, Pallas kernels for 42%

profile of v4, /device:TPU:0, one launch (start us, length us, event | category | flops | bytes accessed | tf_op | source)
XLA Modules:
  0.0 48.1 jit_solution(14047630570742240774)
XLA Ops:
  0.6 1.9 %shard_map.86 = (f32[144,256]{1,0:T(8,128)S(1)}, f32[144,256]{1,0:T(8,128)S(1)}, f32[144,128]{1,0:T(8,128)S(1)}, f32[144,128]{1,0:T(8,128)S(1)}, bf16[1024,768]{...) custom-call(f32[3,48,1024]{2,1,0:T(8,128)} %bitcast.7, ...), custom_call_target="tpu_custom_call" | custom-call | bytes 1048576 | tf_op jit(solution)/shard_map/pallas_call | solution.py:347
  2.6 0.5 %collective-permute-start.2 = (f32[144,128]{1,0:T(8,128)S(1)}, f32[144,128]{1,0:T(8,128)S(1)}, u32[]{:S(2)}, u32[]{:S(2)}) collective-permute-start(f32[144,128]{1,0:T(8,128)S(1)} %get-tuple-element.41), channel_id=1, source_target_pairs={{0,8},{8,0},{16,24},{24,16},{1,9},{9,1},{17,25},{25,17},{2,10},{10... | collective-permute-start | bytes 221192 | tf_op jit(solution)/shard_map/ppermute | solution.py:40
  3.1 2.6 %collective-permute-start.3 = (f32[144,128]{1,0:T(8,128)S(1)}, f32[144,128]{1,0:T(8,128)S(1)}, u32[]{:S(2)}, u32[]{:S(2)}) collective-permute-start(f32[144,128]{1,0:T(8,128)S(1)} %get-tuple-element.42), channel_id=1, source_target_pairs={{0,24},{8,16},{16,8},{24,0},{1,25},{9,17},{17,9},{25,1},{2,26},{10... | collective-permute-start | bytes 221192 | tf_op jit(solution)/shard_map/ppermute | solution.py:40
  5.7 1.5 %collective-permute-start = (f32[144,256]{1,0:T(8,128)S(1)}, f32[144,256]{1,0:T(8,128)S(1)}, u32[]{:S(2)}, u32[]{:S(2)}) collective-permute-start(f32[144,256]{1,0:T(8,128)S(1)} %get-tuple-element.39), channel_id=1, source_target_pairs={{0,1},{1,0},{2,3},{3,2},{4,5},{5,4},{6,7},{7,6},{8,9},{9,8},{10,11... | collective-permute-start | bytes 442376 | tf_op jit(solution)/shard_map/ppermute | solution.py:40
  7.2 0.7 %collective-permute-start.1 = (f32[144,256]{1,0:T(8,128)S(1)}, f32[144,256]{1,0:T(8,128)S(1)}, u32[]{:S(2)}, u32[]{:S(2)}) collective-permute-start(f32[144,256]{1,0:T(8,128)S(1)} %get-tuple-element.40), channel_id=1, source_target_pairs={{1,2},{2,1},{3,4},{4,3},{5,6},{6,5},{9,10},{10,9},{11,12},{12,11},... | collective-permute-start | bytes 442376 | tf_op jit(solution)/shard_map/ppermute | solution.py:40
  7.9 0.0 copy-start
  7.9 10.4 %shard_map.87 = (bf16[1024,768]{1,0:T(8,128)(2,1)S(1)}, bf16[1024,768]{1,0:T(8,128)(2,1)S(1)}, bf16[1024,768]{1,0:T(8,128)(2,1)S(1)}, bf16[1024,768]{1,0:T(8,128...) custom-call(bf16[288,1024]{1,0:T(8,128)(2,1)S(1)} %get-tuple-element, ...), custom_call_target="tpu_custom_call" | custom-call | flops 2717908992 | bytes 1048576 | tf_op jit(solution)/shard_map/pallas_call | solution.py:347
  18.3 0.0 collective-permute-done.2.c_ref
  18.3 0.0 collective-permute-done.3.d_ref
  18.4 0.0 collective-permute-done.a_ref
  18.4 0.0 collective-permute-done.1.b_ref
  18.4 0.0 copy-done
  18.4 5.1 %shard_map.88 = (bf16[4,384,768]{2,1,0:T(8,128)(2,1)S(1)}, f32[48,64]{1,0:T(8,128)S(1)}) custom-call(f32[48,64]{1,0:T(8,128)S(1)} %bitcast.5, f32[2,1024]{1,0:T(2,128)S(1)} %get-tuple-element.34.lame_ref, f32[4,144,768]{2,1,0:T(8,128)S(1)} %get-tuple-element.38.own_ref, f32[144,256]{1,0:T(8,128)S(1)} %collective-permute-done.a_ref, ...), custom_call_target="tpu_custom_call" | custom-call | bytes 1048576 | tf_op jit(solution)/shard_map/pallas_call | solution.py:347
  23.5 4.3 %collective-permute-start.4 = (f32[48,64]{1,0:T(8,128)S(1)}, f32[48,64]{1,0:T(8,128)S(1)}, u32[]{:S(2)}, u32[]{:S(2)}) collective-permute-start(f32[48,64]{1,0:T(8,128)S(1)} %get-tuple-element.52.a_ref), channel_id=1, source_target_pairs={{0,1},{1,0},{2,3},{3,2},{4,5},{5,4},{6,7},{7,6},{8,9},{9,8},{10,11... | collective-permute-start | bytes 36872 | tf_op jit(solution)/shard_map/ppermute | solution.py:434
  27.8 3.4 %shard_map.89 = (f32[192,256]{1,0:T(8,128)S(1)}, f32[192,256]{1,0:T(8,128)S(1)}, f32[240,128]{1,0:T(8,128)S(1)}, f32[240,128]{1,0:T(8,128)S(1)}) custom-call(bf16[4,384,768]{2,1,0:T(8,128)(2,1)S(1)} %get-tuple-element.51.pio_ref, bf16[768,768]{1,0:T(8,128)(2,1)S(1)} %get-tuple-element.43.refs_0_, bf16[768,768]{1,0:T(8,128)(2,1)S(1)} %get-tuple-element.44.refs_1_, ...), custom_call_target="tpu_custom_call" | custom-call | flops 2717908992 | bytes 1048576 | tf_op jit(solution)/shard_map/pallas_call | solution.py:347
  31.2 0.0 collective-permute-done.4.b_ref
  31.2 0.1 collective-permute-start.5
  31.3 0.4 collective-permute-start.7
  31.7 0.9 %collective-permute-done.5.got_ref.c_ref = f32[240,128]{1,0:T(8,128)S(1)} collective-permute-done((f32[240,128]{1,0:T(8,128)S(1)}, f32[240,128]{1,0:T(8,128)S(1)}, u32[]{:S(2)}, u32[]{:S(2)}) %collective-permute-start.5) | collective-permute-done | bytes 122912 | tf_op jit(solution)/shard_map/ppermute | solution.py:40
  32.7 0.3 collective-permute-start.6
  32.9 0.8 %collective-permute-start.8 = (f32[192,256]{1,0:T(8,128)S(1)}, f32[192,256]{1,0:T(8,128)S(1)}, u32[]{:S(2)}, u32[]{:S(2)}) collective-permute-start(f32[192,256]{1,0:T(8,128)S(1)} %shard_map.95), channel_id=1, source_target_pairs={{1,2},{2,1},{3,4},{4,3},{5,6},{6,5},{9,10},{10,9},{11,12},{12,11},... | collective-permute-start | bytes 589832 | tf_op jit(solution)/shard_map/ppermute | solution.py:40
  33.8 2.4 %shard_map.92.refs_0_.refs_4_ = f32[192,1024]{1,0:T(8,128)S(1)} custom-call(bf16[4,384,768]{2,1,0:T(8,128)(2,1)S(1)} %get-tuple-element.51.pio_ref, f32[240,128]{1,0:T(8,128)S(1)} %shard_map.91.after_ref.sent_ref, bf16[1024,768]{1,0:T(8,128)(2,1)S(1)} %get-tuple-element.55.refs_0_, bf16[1024,768]{1,0:T(8,128)(2,1)S(1)} %get-tuple-element.56.refs_1_, ...), custom_call_target="tpu_custom_call" | custom-call | flops 1811939328 | bytes 1048576 | tf_op jit(solution)/shard_map/pallas_call | solution.py:347
  36.2 1.8 %collective-permute-done.6.got_ref.d_ref = f32[240,128]{1,0:T(8,128)S(1)} collective-permute-done((f32[240,128]{1,0:T(8,128)S(1)}, f32[240,128]{1,0:T(8,128)S(1)}, u32[]{:S(2)}, u32[]{:S(2)}) %collective-permute-start.6) | collective-permute-done | bytes 122912 | tf_op jit(solution)/shard_map/ppermute | solution.py:40
  37.9 1.9 %collective-permute-start.9 = (f32[48,64]{1,0:T(8,128)S(1)}, f32[48,64]{1,0:T(8,128)S(1)}, u32[]{:S(2)}, u32[]{:S(2)}) collective-permute-start(f32[48,64]{1,0:T(8,128)S(1)} %shard_map.93.after_ref.a_ref), channel_id=1, source_target_pairs={{0,2},{1,3},{2,0},{3,1},{4,6},{5,7},{6,4},{7,5},{8,10},{9,11},{10,... | collective-permute-start | bytes 36872 | tf_op jit(solution)/shard_map/ppermute | solution.py:434
  39.8 2.4 %shard_map.94.own_ref.refs_0_ = f32[192,1024]{1,0:T(8,128)S(1)} custom-call(bf16[4,384,768]{2,1,0:T(8,128)(2,1)S(1)} %get-tuple-element.51.pio_ref, f32[48,64]{1,0:T(8,128)S(1)} %shard_map.93.after_ref.a_ref, bf16[1024,768]{1,0:T(8,128)(2,1)S(1)} %get-tuple-element.59.refs_0_, bf16[1024,768]{1,0:T(8,128)(2,1)S(1)} %get-tuple-element.60.refs_1_, ...), custom_call_target="tpu_custom_call" | custom-call | flops 1811939328 | bytes 1048576 | tf_op jit(solution)/shard_map/pallas_call | solution.py:347
  42.2 0.6 %collective-permute-done.9.b_ref = f32[48,64]{1,0:T(8,128)S(1)} collective-permute-done((f32[48,64]{1,0:T(8,128)S(1)}, f32[48,64]{1,0:T(8,128)S(1)}, u32[]{:S(2)}, u32[]{:S(2)}) %collective-permute-start.9) | collective-permute-done | bytes 12320 | tf_op jit(solution)/shard_map/ppermute | solution.py:434
  42.8 2.6 %collective-permute-start.10 = (f32[48,64]{1,0:T(8,128)S(1)}, f32[48,64]{1,0:T(8,128)S(1)}, u32[]{:S(2)}, u32[]{:S(2)}) collective-permute-start(f32[48,64]{1,0:T(8,128)S(1)} %shard_map.97.a_ref), channel_id=1, source_target_pairs={{0,4},{1,5},{2,6},{3,7},{4,0},{5,1},{6,2},{7,3},{8,12},{9,13},{10,... | collective-permute-start | bytes 36872 | tf_op jit(solution)/shard_map/ppermute | solution.py:434
  45.4 0.0 collective-permute-done.7.a_ref
  45.4 0.0 collective-permute-done.8.b_ref
  45.4 1.6 %shard_map.96.refs_0_ = f32[3,64,1024]{2,1,0:T(8,128)} custom-call(f32[192,1024]{1,0:T(8,128)S(1)} %shard_map.94.own_ref.refs_0_, bf16[1024,768]{1,0:T(8,128)(2,1)S(1)} %get-tuple-element.63.hot_ref, f32[192,256]{1,0:T(8,128)S(1)} %collective-permute-done.7.a_ref, f32[192,256]{1,0:T(8,128)S(1)} %collective-permute-done.8.b_ref, ...), custom_call_target="tpu_custom_call" | custom-call | bytes 1048576 | tf_op jit(solution)/shard_map/pallas_call | solution.py:347
  47.0 0.5 %collective-permute-done.10.b_ref = f32[48,64]{1,0:T(8,128)S(1)} collective-permute-done((f32[48,64]{1,0:T(8,128)S(1)}, f32[48,64]{1,0:T(8,128)S(1)}, u32[]{:S(2)}, u32[]{:S(2)}) %collective-permute-start.10) | collective-permute-done | bytes 12320 | tf_op jit(solution)/shard_map/ppermute | solution.py:434
  47.5 0.6 %shard_map.98 = f32[48,64]{1,0:T(8,128)} custom-call(f32[48,64]{1,0:T(8,128)S(1)} %shard_map.97.a_ref, f32[48,64]{1,0:T(8,128)S(1)} %collective-permute-done.10.b_ref, f32[3,64,1024]{2,1,0:T(8,128)} %shard_map.96.refs_0_), custom_call_target="tpu_custom_call" | custom-call | bytes 1048576 | tf_op jit(solution)/shard_map/pallas_call | solution.py:347
  (5 shorter events, 0.0 us)
Async XLA Ops:
  2.6 15.8 %collective-permute-start.2 = (f32[144,128]{1,0:T(8,128)S(1)}, f32[144,128]{1,0:T(8,128)S(1)}, u32[]{:S(2)}, u32[]{:S(2)}) collective-permute-start(f32[144,128]{1,0:T(8,128)S(1)} %get-tuple-element.41), channel_id=1, source_target_pairs={{0,8},{8,0},{16,24},{24,16},{1,9},{9,1},{17,25},{25,17},{2,10},{10... | collective-permute-start | bytes 221192 | tf_op jit(solution)/shard_map/ppermute | solution.py:40
  3.1 15.3 %collective-permute-start.3 = (f32[144,128]{1,0:T(8,128)S(1)}, f32[144,128]{1,0:T(8,128)S(1)}, u32[]{:S(2)}, u32[]{:S(2)}) collective-permute-start(f32[144,128]{1,0:T(8,128)S(1)} %get-tuple-element.42), channel_id=1, source_target_pairs={{0,24},{8,16},{16,8},{24,0},{1,25},{9,17},{17,9},{25,1},{2,26},{10... | collective-permute-start | bytes 221192 | tf_op jit(solution)/shard_map/ppermute | solution.py:40
  5.7 12.6 %collective-permute-start = (f32[144,256]{1,0:T(8,128)S(1)}, f32[144,256]{1,0:T(8,128)S(1)}, u32[]{:S(2)}, u32[]{:S(2)}) collective-permute-start(f32[144,256]{1,0:T(8,128)S(1)} %get-tuple-element.39), channel_id=1, source_target_pairs={{0,1},{1,0},{2,3},{3,2},{4,5},{5,4},{6,7},{7,6},{8,9},{9,8},{10,11... | collective-permute-start | bytes 442376 | tf_op jit(solution)/shard_map/ppermute | solution.py:40
  7.2 11.1 %collective-permute-start.1 = (f32[144,256]{1,0:T(8,128)S(1)}, f32[144,256]{1,0:T(8,128)S(1)}, u32[]{:S(2)}, u32[]{:S(2)}) collective-permute-start(f32[144,256]{1,0:T(8,128)S(1)} %get-tuple-element.40), channel_id=1, source_target_pairs={{1,2},{2,1},{3,4},{4,3},{5,6},{6,5},{9,10},{10,9},{11,12},{12,11},... | collective-permute-start | bytes 442376 | tf_op jit(solution)/shard_map/ppermute | solution.py:40
  7.9 10.5 %copy-start = (f32[64,48]{0,1:T(8,128)S(1)}, f32[64,48]{0,1:T(8,128)}, u32[]{:S(2)}) copy-start(f32[64,48]{0,1:T(8,128)} %param.7) | copy-start | bytes 36868
  23.5 7.7 %collective-permute-start.4 = (f32[48,64]{1,0:T(8,128)S(1)}, f32[48,64]{1,0:T(8,128)S(1)}, u32[]{:S(2)}, u32[]{:S(2)}) collective-permute-start(f32[48,64]{1,0:T(8,128)S(1)} %get-tuple-element.52.a_ref), channel_id=1, source_target_pairs={{0,1},{1,0},{2,3},{3,2},{4,5},{5,4},{6,7},{7,6},{8,9},{9,8},{10,11... | collective-permute-start | bytes 36872 | tf_op jit(solution)/shard_map/ppermute | solution.py:434
  31.2 1.4 %collective-permute-start.5 = (f32[240,128]{1,0:T(8,128)S(1)}, f32[240,128]{1,0:T(8,128)S(1)}, u32[]{:S(2)}, u32[]{:S(2)}) collective-permute-start(f32[240,128]{1,0:T(8,128)S(1)} %shard_map.90.sent_ref), channel_id=1, source_target_pairs={{0,8},{8,0},{16,24},{24,16},{1,9},{9,1},{17,25},{25,17},{2,10},{10... | collective-permute-start | bytes 368648 | tf_op jit(solution)/shard_map/ppermute | solution.py:40
  31.3 14.1 %collective-permute-start.7 = (f32[192,256]{1,0:T(8,128)S(1)}, f32[192,256]{1,0:T(8,128)S(1)}, u32[]{:S(2)}, u32[]{:S(2)}) collective-permute-start(f32[192,256]{1,0:T(8,128)S(1)} %get-tuple-element.64), channel_id=1, source_target_pairs={{0,1},{1,0},{2,3},{3,2},{4,5},{5,4},{6,7},{7,6},{8,9},{9,8},{10,11... | collective-permute-start | bytes 589832 | tf_op jit(solution)/shard_map/ppermute | solution.py:40
  32.7 5.3 %collective-permute-start.6 = (f32[240,128]{1,0:T(8,128)S(1)}, f32[240,128]{1,0:T(8,128)S(1)}, u32[]{:S(2)}, u32[]{:S(2)}) collective-permute-start(f32[240,128]{1,0:T(8,128)S(1)} %shard_map.91.after_ref.sent_ref), channel_id=1, source_target_pairs={{0,24},{8,16},{16,8},{24,0},{1,25},{9,17},{17,9},{25,1},{2,26},{10... | collective-permute-start | bytes 368648 | tf_op jit(solution)/shard_map/ppermute | solution.py:40
  32.9 12.5 %collective-permute-start.8 = (f32[192,256]{1,0:T(8,128)S(1)}, f32[192,256]{1,0:T(8,128)S(1)}, u32[]{:S(2)}, u32[]{:S(2)}) collective-permute-start(f32[192,256]{1,0:T(8,128)S(1)} %shard_map.95), channel_id=1, source_target_pairs={{1,2},{2,1},{3,4},{4,3},{5,6},{6,5},{9,10},{10,9},{11,12},{12,11},... | collective-permute-start | bytes 589832 | tf_op jit(solution)/shard_map/ppermute | solution.py:40
  37.9 4.8 %collective-permute-start.9 = (f32[48,64]{1,0:T(8,128)S(1)}, f32[48,64]{1,0:T(8,128)S(1)}, u32[]{:S(2)}, u32[]{:S(2)}) collective-permute-start(f32[48,64]{1,0:T(8,128)S(1)} %shard_map.93.after_ref.a_ref), channel_id=1, source_target_pairs={{0,2},{1,3},{2,0},{3,1},{4,6},{5,7},{6,4},{7,5},{8,10},{9,11},{10,... | collective-permute-start | bytes 36872 | tf_op jit(solution)/shard_map/ppermute | solution.py:434
  42.8 4.7 %collective-permute-start.10 = (f32[48,64]{1,0:T(8,128)S(1)}, f32[48,64]{1,0:T(8,128)S(1)}, u32[]{:S(2)}, u32[]{:S(2)}) collective-permute-start(f32[48,64]{1,0:T(8,128)S(1)} %shard_map.97.a_ref), channel_id=1, source_target_pairs={{0,4},{1,5},{2,6},{3,7},{4,0},{5,1},{6,2},{7,3},{8,12},{9,13},{10,... | collective-permute-start | bytes 36872 | tf_op jit(solution)/shard_map/ppermute | solution.py:434

commit v5 on v4

--- a/solution.py
+++ b/solution.py
@@ -312,12 +312,24 @@
             out_ref[...] += part
 
 
-def add_kernel(own_ref, hot_ref, a_ref, b_ref, c_ref, d_ref, out_hbm, back, out_s, sems):
+def rest_kernel(pio_ref, after_ref, hot_ref, c_ref, d_ref, *refs, first):
+    own_kernel(pio_ref, after_ref, *refs, first=first)
+    out_ref = refs[-1]
+    rows = out_ref.shape[0]
+    col = hot_ref.shape[1] - c_ref.shape[1] - d_ref.shape[1]
+    for r in (c_ref, d_ref):
+        both = jnp.concatenate(split(r[0:rows, :]), axis=0)
+        part = dot(both, hot_ref[:, col : col + r.shape[1]], NT)
+        out_ref[...] += part[:rows] + part[rows:]
+        col += r.shape[1]
+
+
+def add_kernel(own_ref, hot_ref, a_ref, b_ref, out_hbm, back, out_s, sems):
     node_total = own_ref.shape[1]
     rows = own_ref.shape[0]
     combos = rows // 3
     col = 0
-    for r in (a_ref, b_ref, c_ref, d_ref):
+    for r in (a_ref, b_ref):
         hi, lo = split(r[0:rows, :])
         back[0:rows, col : col + r.shape[1]] = hi
         back[rows:, col : col + r.shape[1]] = lo
@@ -326,7 +338,7 @@
     for k in range(sems.shape[0]):
         width = node_total // sems.shape[0]
         at = slice(k * width, (k + 1) * width)
-        part = dot(back[...], hot_ref[at, :], NT)
+        part = dot(back[...], hot_ref[at, 0:col], NT)
         for i in range(3):
             r = slice(i * combos, (i + 1) * combos)
             low = slice(rows + i * combos, rows + (i + 1) * combos)
@@ -484,7 +496,14 @@
         (*landed, own),
         any_in=(2,),
     )
-    own = scatter_own(chunks // 2, chunks, modal, (own,))
+    mid = chunks // 2
+    own = call(
+        functools.partial(rest_kernel, first=mid),
+        sds((rows, node_total), F32),
+        (pio, modal, hot, got_c, got_d, *elem[mid:chunks], *elem[chunks + mid : 2 * chunks], own),
+        any_in=(1,),
+        flops=2 * 3 * rows * node_total * 3 * LANES * (chunks - mid),
+    )
     step = 2
     while not ride and step < sector:
         modal = modal + other(modal, "sector", step)
@@ -493,13 +512,13 @@
     while 4 * step <= dom:
         modal = fold(modal, "dom", step, own)
         step *= 2
-    returned = (got_a, got_b, got_c, got_d)
+    returned = (got_a, got_b)
     forces = call(
         add_kernel,
         sds((3, combos, node_total), F32),
         (own, hot, *returned),
         scratch=[
-            pltpu.VMEM((6 * combos, halo_width), BF16),
+            pltpu.VMEM((6 * combos, 2 * dom_width), BF16),
             pltpu.VMEM((3, combos, node_total), F32),
             pltpu.SemaphoreType.DMA((4,)),
         ],

time: 48.3 us -> 48.3 us (level)
  no operation moved by 1% of the time
where the time goes in v5:
time: 48.3 us; the launch traced here: 48.1 us
  Pallas kernels  28.1 us (58%)
  starting transfers between devices  15.7 us (33%)
  waiting for transfers between devices  3.6 us (7%)
  between operations  0.77 us (2%)
    pallas_call x13, Pallas kernels, call(): pl.pallas_call(kernel, out_shape=out_shape, in_specs=[hbm if i in hbm_in...  28.1 us
    ppermute x3, starting transfers between devices, other(): lax.ppermute(x, axis, [(i, i ^ step) for i in range(lax.axis_size(axis))])  8.75 us
    ppermute x8, starting transfers between devices, swap(): return lax.ppermute(x, axis, [(i, j % count) for i, j in pairs])  6.9 us
    ppermute x8, waiting for transfers between devices, swap(): return lax.ppermute(x, axis, [(i, j % count) for i, j in pairs])  2.71 us
  transfers between devices with their start and end apart: 11, of which 4 were waited for; matrix products, arithmetic and copies ran while one was open for 0% of the time, Pallas kernels for 42%

profile of v5, /device:TPU:0, one launch (start us, length us, event | category | flops | bytes accessed | tf_op | source)
XLA Modules:
  0.0 48.1 jit_solution(6665110027642807306)
XLA Ops:
  0.6 1.9 %shard_map.86 = (f32[144,256]{1,0:T(8,128)S(1)}, f32[144,256]{1,0:T(8,128)S(1)}, f32[144,128]{1,0:T(8,128)S(1)}, f32[144,128]{1,0:T(8,128)S(1)}, bf16[1024,768]{...) custom-call(f32[3,48,1024]{2,1,0:T(8,128)} %bitcast.7, ...), custom_call_target="tpu_custom_call" | custom-call | bytes 1048576 | tf_op jit(solution)/shard_map/pallas_call | solution.py:359
  2.6 0.5 %collective-permute-start.2 = (f32[144,128]{1,0:T(8,128)S(1)}, f32[144,128]{1,0:T(8,128)S(1)}, u32[]{:S(2)}, u32[]{:S(2)}) collective-permute-start(f32[144,128]{1,0:T(8,128)S(1)} %get-tuple-element.41), channel_id=1, source_target_pairs={{0,8},{8,0},{16,24},{24,16},{1,9},{9,1},{17,25},{25,17},{2,10},{10... | collective-permute-start | bytes 221192 | tf_op jit(solution)/shard_map/ppermute | solution.py:40
  3.1 2.6 %collective-permute-start.3 = (f32[144,128]{1,0:T(8,128)S(1)}, f32[144,128]{1,0:T(8,128)S(1)}, u32[]{:S(2)}, u32[]{:S(2)}) collective-permute-start(f32[144,128]{1,0:T(8,128)S(1)} %get-tuple-element.42), channel_id=1, source_target_pairs={{0,24},{8,16},{16,8},{24,0},{1,25},{9,17},{17,9},{25,1},{2,26},{10... | collective-permute-start | bytes 221192 | tf_op jit(solution)/shard_map/ppermute | solution.py:40
  5.7 1.5 %collective-permute-start = (f32[144,256]{1,0:T(8,128)S(1)}, f32[144,256]{1,0:T(8,128)S(1)}, u32[]{:S(2)}, u32[]{:S(2)}) collective-permute-start(f32[144,256]{1,0:T(8,128)S(1)} %get-tuple-element.39), channel_id=1, source_target_pairs={{0,1},{1,0},{2,3},{3,2},{4,5},{5,4},{6,7},{7,6},{8,9},{9,8},{10,11... | collective-permute-start | bytes 442376 | tf_op jit(solution)/shard_map/ppermute | solution.py:40
  7.2 0.7 %collective-permute-start.1 = (f32[144,256]{1,0:T(8,128)S(1)}, f32[144,256]{1,0:T(8,128)S(1)}, u32[]{:S(2)}, u32[]{:S(2)}) collective-permute-start(f32[144,256]{1,0:T(8,128)S(1)} %get-tuple-element.40), channel_id=1, source_target_pairs={{1,2},{2,1},{3,4},{4,3},{5,6},{6,5},{9,10},{10,9},{11,12},{12,11},... | collective-permute-start | bytes 442376 | tf_op jit(solution)/shard_map/ppermute | solution.py:40
  7.9 0.0 copy-start
  7.9 10.4 %shard_map.87 = (bf16[1024,768]{1,0:T(8,128)(2,1)S(1)}, bf16[1024,768]{1,0:T(8,128)(2,1)S(1)}, bf16[1024,768]{1,0:T(8,128)(2,1)S(1)}, bf16[1024,768]{1,0:T(8,128...) custom-call(bf16[288,1024]{1,0:T(8,128)(2,1)S(1)} %get-tuple-element, ...), custom_call_target="tpu_custom_call" | custom-call | flops 2717908992 | bytes 1048576 | tf_op jit(solution)/shard_map/pallas_call | solution.py:359
  18.3 0.0 collective-permute-done.2.c_ref
  18.4 0.0 collective-permute-done.3.d_ref
  18.4 0.0 collective-permute-done.a_ref
  18.4 0.0 collective-permute-done.1.b_ref
  18.4 0.0 copy-done
  18.4 5.1 %shard_map.88 = (bf16[4,384,768]{2,1,0:T(8,128)(2,1)S(1)}, f32[48,64]{1,0:T(8,128)S(1)}) custom-call(f32[48,64]{1,0:T(8,128)S(1)} %bitcast.5, f32[2,1024]{1,0:T(2,128)S(1)} %get-tuple-element.34.lame_ref, f32[4,144,768]{2,1,0:T(8,128)S(1)} %get-tuple-element.38.own_ref, f32[144,256]{1,0:T(8,128)S(1)} %collective-permute-done.a_ref, ...), custom_call_target="tpu_custom_call" | custom-call | bytes 1048576 | tf_op jit(solution)/shard_map/pallas_call | solution.py:359
  23.5 4.3 %collective-permute-start.4 = (f32[48,64]{1,0:T(8,128)S(1)}, f32[48,64]{1,0:T(8,128)S(1)}, u32[]{:S(2)}, u32[]{:S(2)}) collective-permute-start(f32[48,64]{1,0:T(8,128)S(1)} %get-tuple-element.52.a_ref), channel_id=1, source_target_pairs={{0,1},{1,0},{2,3},{3,2},{4,5},{5,4},{6,7},{7,6},{8,9},{9,8},{10,11... | collective-permute-start | bytes 36872 | tf_op jit(solution)/shard_map/ppermute | solution.py:446
  27.8 3.4 %shard_map.89 = (f32[192,256]{1,0:T(8,128)S(1)}, f32[192,256]{1,0:T(8,128)S(1)}, f32[240,128]{1,0:T(8,128)S(1)}, f32[240,128]{1,0:T(8,128)S(1)}) custom-call(bf16[4,384,768]{2,1,0:T(8,128)(2,1)S(1)} %get-tuple-element.51.pio_ref, bf16[768,768]{1,0:T(8,128)(2,1)S(1)} %get-tuple-element.43.refs_0_, bf16[768,768]{1,0:T(8,128)(2,1)S(1)} %get-tuple-element.44.refs_1_, ...), custom_call_target="tpu_custom_call" | custom-call | flops 2717908992 | bytes 1048576 | tf_op jit(solution)/shard_map/pallas_call | solution.py:359
  31.2 0.0 collective-permute-done.4.b_ref
  31.3 0.1 collective-permute-start.5
  31.3 0.4 collective-permute-start.7
  31.8 0.9 %collective-permute-done.5.got_ref.c_ref = f32[240,128]{1,0:T(8,128)S(1)} collective-permute-done((f32[240,128]{1,0:T(8,128)S(1)}, f32[240,128]{1,0:T(8,128)S(1)}, u32[]{:S(2)}, u32[]{:S(2)}) %collective-permute-start.5) | collective-permute-done | bytes 122912 | tf_op jit(solution)/shard_map/ppermute | solution.py:40
  32.7 0.3 collective-permute-start.6
  32.9 0.8 %collective-permute-start.8 = (f32[192,256]{1,0:T(8,128)S(1)}, f32[192,256]{1,0:T(8,128)S(1)}, u32[]{:S(2)}, u32[]{:S(2)}) collective-permute-start(f32[192,256]{1,0:T(8,128)S(1)} %shard_map.95), channel_id=1, source_target_pairs={{1,2},{2,1},{3,4},{4,3},{5,6},{6,5},{9,10},{10,9},{11,12},{12,11},... | collective-permute-start | bytes 589832 | tf_op jit(solution)/shard_map/ppermute | solution.py:40
  33.8 2.4 %shard_map.92.refs_0_.refs_4_ = f32[192,1024]{1,0:T(8,128)S(1)} custom-call(bf16[4,384,768]{2,1,0:T(8,128)(2,1)S(1)} %get-tuple-element.51.pio_ref, f32[240,128]{1,0:T(8,128)S(1)} %shard_map.91.after_ref.sent_ref, bf16[1024,768]{1,0:T(8,128)(2,1)S(1)} %get-tuple-element.55.refs_0_, bf16[1024,768]{1,0:T(8,128)(2,1)S(1)} %get-tuple-element.56.refs_1_, ...), custom_call_target="tpu_custom_call" | custom-call | flops 1811939328 | bytes 1048576 | tf_op jit(solution)/shard_map/pallas_call | solution.py:359
  36.2 1.8 %collective-permute-done.6.got_ref.d_ref = f32[240,128]{1,0:T(8,128)S(1)} collective-permute-done((f32[240,128]{1,0:T(8,128)S(1)}, f32[240,128]{1,0:T(8,128)S(1)}, u32[]{:S(2)}, u32[]{:S(2)}) %collective-permute-start.6) | collective-permute-done | bytes 122912 | tf_op jit(solution)/shard_map/ppermute | solution.py:40
  38.0 1.9 %collective-permute-start.9 = (f32[48,64]{1,0:T(8,128)S(1)}, f32[48,64]{1,0:T(8,128)S(1)}, u32[]{:S(2)}, u32[]{:S(2)}) collective-permute-start(f32[48,64]{1,0:T(8,128)S(1)} %shard_map.93.after_ref.a_ref), channel_id=1, source_target_pairs={{0,2},{1,3},{2,0},{3,1},{4,6},{5,7},{6,4},{7,5},{8,10},{9,11},{10,... | collective-permute-start | bytes 36872 | tf_op jit(solution)/shard_map/ppermute | solution.py:446
  39.8 2.8 %shard_map.94.own_ref.refs_0_ = f32[192,1024]{1,0:T(8,128)S(1)} custom-call(bf16[4,384,768]{2,1,0:T(8,128)(2,1)S(1)} %get-tuple-element.51.pio_ref, f32[48,64]{1,0:T(8,128)S(1)} %shard_map.93.after_ref.a_ref, bf16[1024,768]{1,0:T(8,128)(2,1)S(1)} %get-tuple-element.59.hot_ref, f32[240,128]{1,0:T(8,128)S(1)} %collective-permute-done.5.got_ref.c_ref, ...), custom_call_target="tpu_custom_call" | custom-call | flops 1811939328 | bytes 1048576 | tf_op jit(solution)/shard_map/pallas_call | solution.py:359
  42.6 0.2 collective-permute-done.9.b_ref
  42.8 2.6 %collective-permute-start.10 = (f32[48,64]{1,0:T(8,128)S(1)}, f32[48,64]{1,0:T(8,128)S(1)}, u32[]{:S(2)}, u32[]{:S(2)}) collective-permute-start(f32[48,64]{1,0:T(8,128)S(1)} %shard_map.97.a_ref), channel_id=1, source_target_pairs={{0,4},{1,5},{2,6},{3,7},{4,0},{5,1},{6,2},{7,3},{8,12},{9,13},{10,... | collective-permute-start | bytes 36872 | tf_op jit(solution)/shard_map/ppermute | solution.py:446
  45.4 0.0 collective-permute-done.7.a_ref
  45.4 0.0 collective-permute-done.8.b_ref
  45.4 1.4 %shard_map.96.refs_0_ = f32[3,64,1024]{2,1,0:T(8,128)} custom-call(f32[192,1024]{1,0:T(8,128)S(1)} %shard_map.94.own_ref.refs_0_, bf16[1024,768]{1,0:T(8,128)(2,1)S(1)} %get-tuple-element.59.hot_ref, f32[192,256]{1,0:T(8,128)S(1)} %collective-permute-done.7.a_ref, f32[192,256]{1,0:T(8,128)S(1)} %collective-permute-done.8.b_ref), custom_call_target="tpu_custom_call" | custom-call | bytes 1048576 | tf_op jit(solution)/shard_map/pallas_call | solution.py:359
  46.8 0.7 %collective-permute-done.10.b_ref = f32[48,64]{1,0:T(8,128)S(1)} collective-permute-done((f32[48,64]{1,0:T(8,128)S(1)}, f32[48,64]{1,0:T(8,128)S(1)}, u32[]{:S(2)}, u32[]{:S(2)}) %collective-permute-start.10) | collective-permute-done | bytes 12320 | tf_op jit(solution)/shard_map/ppermute | solution.py:446
  47.5 0.6 %shard_map.98 = f32[48,64]{1,0:T(8,128)} custom-call(f32[48,64]{1,0:T(8,128)S(1)} %shard_map.97.a_ref, f32[48,64]{1,0:T(8,128)S(1)} %collective-permute-done.10.b_ref, f32[3,64,1024]{2,1,0:T(8,128)} %shard_map.96.refs_0_), custom_call_target="tpu_custom_call" | custom-call | bytes 1048576 | tf_op jit(solution)/shard_map/pallas_call | solution.py:359
  (5 shorter events, 0.0 us)
Async XLA Ops:
  2.6 15.8 %collective-permute-start.2 = (f32[144,128]{1,0:T(8,128)S(1)}, f32[144,128]{1,0:T(8,128)S(1)}, u32[]{:S(2)}, u32[]{:S(2)}) collective-permute-start(f32[144,128]{1,0:T(8,128)S(1)} %get-tuple-element.41), channel_id=1, source_target_pairs={{0,8},{8,0},{16,24},{24,16},{1,9},{9,1},{17,25},{25,17},{2,10},{10... | collective-permute-start | bytes 221192 | tf_op jit(solution)/shard_map/ppermute | solution.py:40
  3.1 15.3 %collective-permute-start.3 = (f32[144,128]{1,0:T(8,128)S(1)}, f32[144,128]{1,0:T(8,128)S(1)}, u32[]{:S(2)}, u32[]{:S(2)}) collective-permute-start(f32[144,128]{1,0:T(8,128)S(1)} %get-tuple-element.42), channel_id=1, source_target_pairs={{0,24},{8,16},{16,8},{24,0},{1,25},{9,17},{17,9},{25,1},{2,26},{10... | collective-permute-start | bytes 221192 | tf_op jit(solution)/shard_map/ppermute | solution.py:40
  5.7 12.6 %collective-permute-start = (f32[144,256]{1,0:T(8,128)S(1)}, f32[144,256]{1,0:T(8,128)S(1)}, u32[]{:S(2)}, u32[]{:S(2)}) collective-permute-start(f32[144,256]{1,0:T(8,128)S(1)} %get-tuple-element.39), channel_id=1, source_target_pairs={{0,1},{1,0},{2,3},{3,2},{4,5},{5,4},{6,7},{7,6},{8,9},{9,8},{10,11... | collective-permute-start | bytes 442376 | tf_op jit(solution)/shard_map/ppermute | solution.py:40
  7.2 11.1 %collective-permute-start.1 = (f32[144,256]{1,0:T(8,128)S(1)}, f32[144,256]{1,0:T(8,128)S(1)}, u32[]{:S(2)}, u32[]{:S(2)}) collective-permute-start(f32[144,256]{1,0:T(8,128)S(1)} %get-tuple-element.40), channel_id=1, source_target_pairs={{1,2},{2,1},{3,4},{4,3},{5,6},{6,5},{9,10},{10,9},{11,12},{12,11},... | collective-permute-start | bytes 442376 | tf_op jit(solution)/shard_map/ppermute | solution.py:40
  7.9 10.5 %copy-start = (f32[64,48]{0,1:T(8,128)S(1)}, f32[64,48]{0,1:T(8,128)}, u32[]{:S(2)}) copy-start(f32[64,48]{0,1:T(8,128)} %param.7) | copy-start | bytes 36868
  23.5 7.7 %collective-permute-start.4 = (f32[48,64]{1,0:T(8,128)S(1)}, f32[48,64]{1,0:T(8,128)S(1)}, u32[]{:S(2)}, u32[]{:S(2)}) collective-permute-start(f32[48,64]{1,0:T(8,128)S(1)} %get-tuple-element.52.a_ref), channel_id=1, source_target_pairs={{0,1},{1,0},{2,3},{3,2},{4,5},{5,4},{6,7},{7,6},{8,9},{9,8},{10,11... | collective-permute-start | bytes 36872 | tf_op jit(solution)/shard_map/ppermute | solution.py:446
  31.3 1.4 %collective-permute-start.5 = (f32[240,128]{1,0:T(8,128)S(1)}, f32[240,128]{1,0:T(8,128)S(1)}, u32[]{:S(2)}, u32[]{:S(2)}) collective-permute-start(f32[240,128]{1,0:T(8,128)S(1)} %shard_map.90.sent_ref), channel_id=1, source_target_pairs={{0,8},{8,0},{16,24},{24,16},{1,9},{9,1},{17,25},{25,17},{2,10},{10... | collective-permute-start | bytes 368648 | tf_op jit(solution)/shard_map/ppermute | solution.py:40
  31.3 14.0 %collective-permute-start.7 = (f32[192,256]{1,0:T(8,128)S(1)}, f32[192,256]{1,0:T(8,128)S(1)}, u32[]{:S(2)}, u32[]{:S(2)}) collective-permute-start(f32[192,256]{1,0:T(8,128)S(1)} %get-tuple-element.64), channel_id=1, source_target_pairs={{0,1},{1,0},{2,3},{3,2},{4,5},{5,4},{6,7},{7,6},{8,9},{9,8},{10,11... | collective-permute-start | bytes 589832 | tf_op jit(solution)/shard_map/ppermute | solution.py:40
  32.7 5.3 %collective-permute-start.6 = (f32[240,128]{1,0:T(8,128)S(1)}, f32[240,128]{1,0:T(8,128)S(1)}, u32[]{:S(2)}, u32[]{:S(2)}) collective-permute-start(f32[240,128]{1,0:T(8,128)S(1)} %shard_map.91.after_ref.sent_ref), channel_id=1, source_target_pairs={{0,24},{8,16},{16,8},{24,0},{1,25},{9,17},{17,9},{25,1},{2,26},{10... | collective-permute-start | bytes 368648 | tf_op jit(solution)/shard_map/ppermute | solution.py:40
  32.9 12.5 %collective-permute-start.8 = (f32[192,256]{1,0:T(8,128)S(1)}, f32[192,256]{1,0:T(8,128)S(1)}, u32[]{:S(2)}, u32[]{:S(2)}) collective-permute-start(f32[192,256]{1,0:T(8,128)S(1)} %shard_map.95), channel_id=1, source_target_pairs={{1,2},{2,1},{3,4},{4,3},{5,6},{6,5},{9,10},{10,9},{11,12},{12,11},... | collective-permute-start | bytes 589832 | tf_op jit(solution)/shard_map/ppermute | solution.py:40
  38.0 4.8 %collective-permute-start.9 = (f32[48,64]{1,0:T(8,128)S(1)}, f32[48,64]{1,0:T(8,128)S(1)}, u32[]{:S(2)}, u32[]{:S(2)}) collective-permute-start(f32[48,64]{1,0:T(8,128)S(1)} %shard_map.93.after_ref.a_ref), channel_id=1, source_target_pairs={{0,2},{1,3},{2,0},{3,1},{4,6},{5,7},{6,4},{7,5},{8,10},{9,11},{10,... | collective-permute-start | bytes 36872 | tf_op jit(solution)/shard_map/ppermute | solution.py:446
  42.8 4.7 %collective-permute-start.10 = (f32[48,64]{1,0:T(8,128)S(1)}, f32[48,64]{1,0:T(8,128)S(1)}, u32[]{:S(2)}, u32[]{:S(2)}) collective-permute-start(f32[48,64]{1,0:T(8,128)S(1)} %shard_map.97.a_ref), channel_id=1, source_target_pairs={{0,4},{1,5},{2,6},{3,7},{4,0},{5,1},{6,2},{7,3},{8,12},{9,13},{10,... | collective-permute-start | bytes 36872 | tf_op jit(solution)/shard_map/ppermute | solution.py:446
